TPU v7x, 32 devices: a whole 2x2x4 slice. The times are simulated.
32 devices in a mesh: cell: 16 (over z, y, x), view: 2 (over core).
Axes of the slice: x: 2, y: 2, z: 4, core: 2. Of those that a mesh axis runs over, the one named last changes fastest.
Arguments:
- gauss_params: float32 [59, 614400], P(None, ('cell', 'view')), as said below
- visible: int32 [4, 614400], P(None, ('cell', 'view')), may hold values 0 or 1
- cameras: float32 [4, 15], replicated, as said below
- tile_ids: int32 [16, 2, 120], P('cell', 'view'), may hold values from 0 to 1919, as said below
- tile_blocks: int32 [16, 2, 120, 2], P('cell', 'view'), may hold values from -1 to 4799, as said below
- target: float32 [2, 3, 256, 1920], P('view', None, 'cell'), as said below
Outputs:
- image: float32 [2, 3, 256, 1920], P('view', None, 'cell')
- loss_map: float32 [2, 256, 1920], P('view', 'cell')
Inputs may be any that keep to these rules, and one draw needn't show every extreme that they name: `tile_ids`: for each view index v the lists of the 16 renderers (c, v) together name each of the 1920 tiles of views 2 v and 2 v + 1 exactly once. The tiles of one renderer lie in 120 different columns t % 120, at most 8 of them in one stripe t // 120, and some renderer reaches 8. `tile_blocks`: an entry names a block g (Gaussians 128 g to 128 g + 127, held by device g // 150 of cell+view) or is -1. The live entries of a tile come first, 1 to 2 of them, and some tile has 2. Every block is named by exactly one tile of all. The live entries of one renderer number exactly 150; at most 5 of them name blocks of one device, and every renderer reaches 5 with some device. `gauss_params`: rows 0 to 2: mean; 3 to 5: logarithms of the scales; 6 to 9: rotation quaternion, real part in row 6 between 1 and 2; row 10: opacity logit, at most 2; row 11 + 3 j + k: coefficient j of the spherical harmonics of colour channel k. Every Gaussian of a block named by a tile lies at depth about 4 to 40 in front of the camera of that tile's view. `cameras`: row w: a rotation (world to camera, row-major) in entries 0 to 8, the translation in 9 to 11, the focal length in pixels in 12 and the principal point (column, row) in 13 and 14. `target`: every value lies between 0.02 and 1.
All inputs are finite; a program needn't handle non-finite values. No bound on the sum of `visible` on one device may be relied on, other than what follows from the above.
Results may differ from a plain program's by a relative error of at most 0.0003.
Values sent between devices are 32-bit elements; how exact they have to be, the bound alone decides.
No kernel may reach another device: no remote copies, remote signals or barrier semaphores. Data moves between devices by JAX's collectives and lax.ppermute only.
A program may use at most 64 MiB of HBM per device.

v0:
```python
import jax
import jax.numpy as jnp
from jax import lax
from jax.sharding import PartitionSpec as P

GBLK = 128


def with_halo(cells, sides, width):
    for axis, dim in sides:
        count = lax.axis_size(axis)
        head = lax.slice_in_dim(cells, 0, width, axis=dim)
        tail = lax.slice_in_dim(cells, cells.shape[dim] - width, cells.shape[dim], axis=dim)
        cells = jnp.concatenate(
            [
                lax.ppermute(tail, axis, [(i, (i + 1) % count) for i in range(count)]),
                cells,
                lax.ppermute(head, axis, [((i + 1) % count, i) for i in range(count)]),
            ],
            axis=dim,
        )
    return cells


def harmonics(unit_x, unit_y, unit_z):
    square_x = unit_x * unit_x
    square_y = unit_y * unit_y
    square_z = unit_z * unit_z
    return [
        0.28209479177387814 + 0.0 * unit_x,
        -0.4886025119029199 * unit_y,
        0.4886025119029199 * unit_z,
        -0.4886025119029199 * unit_x,
        1.0925484305920792 * unit_x * unit_y,
        -1.0925484305920792 * unit_y * unit_z,
        0.31539156525252005 * (2.0 * square_z - square_x - square_y),
        -1.0925484305920792 * unit_x * unit_z,
        0.5462742152960396 * (square_x - square_y),
        -0.5900435899266435 * unit_y * (3.0 * square_x - square_y),
        2.890611442640554 * unit_x * unit_y * unit_z,
        -0.4570457994644658 * unit_y * (4.0 * square_z - square_x - square_y),
        0.3731763325901154 * unit_z * (2.0 * square_z - 3.0 * square_x - 3.0 * square_y),
        -0.4570457994644658 * unit_x * (4.0 * square_z - square_x - square_y),
        1.445305721320277 * unit_z * (square_x - square_y),
        -0.5900435899266435 * unit_x * (square_x - 3.0 * square_y),
    ]


def project(raw_params, camera, seen_mask):
    entries = [camera[:, number][:, None] for number in range(15)]
    rotation = [
        [entries[0], entries[1], entries[2]],
        [entries[3], entries[4], entries[5]],
        [entries[6], entries[7], entries[8]],
    ]
    offset = [entries[9], entries[10], entries[11]]
    focal_len = entries[12]
    centre_pos = [raw_params[:, number] for number in range(3)]
    in_camera = [
        rotation[member][0] * centre_pos[0]
        + rotation[member][1] * centre_pos[1]
        + rotation[member][2] * centre_pos[2]
        + offset[member]
        for member in range(3)
    ]
    depths = in_camera[2]
    screen_x = focal_len * in_camera[0] / depths + entries[13]
    screen_y = focal_len * in_camera[1] / depths + entries[14]
    quaternion = [raw_params[:, 6 + number] for number in range(4)]
    length = jnp.sqrt(
        quaternion[0] * quaternion[0]
        + quaternion[1] * quaternion[1]
        + quaternion[2] * quaternion[2]
        + quaternion[3] * quaternion[3]
    )
    real_part, imag_x, imag_y, imag_z = [part / length for part in quaternion]
    turn_q = [
        [
            1.0 - 2.0 * (imag_y * imag_y + imag_z * imag_z),
            2.0 * (imag_x * imag_y - real_part * imag_z),
            2.0 * (imag_x * imag_z + real_part * imag_y),
        ],
        [
            2.0 * (imag_x * imag_y + real_part * imag_z),
            1.0 - 2.0 * (imag_x * imag_x + imag_z * imag_z),
            2.0 * (imag_y * imag_z - real_part * imag_x),
        ],
        [
            2.0 * (imag_x * imag_z - real_part * imag_y),
            2.0 * (imag_y * imag_z + real_part * imag_x),
            1.0 - 2.0 * (imag_x * imag_x + imag_y * imag_y),
        ],
    ]
    squares = [jnp.exp(2.0 * raw_params[:, 3 + number]) for number in range(3)]
    jacobian = [
        [focal_len / depths, 0.0 * depths, -focal_len * in_camera[0] / (depths * depths)],
        [0.0 * depths, focal_len / depths, -focal_len * in_camera[1] / (depths * depths)],
    ]
    with_cam = [
        [
            jacobian[member][0] * rotation[0][column]
            + jacobian[member][1] * rotation[1][column]
            + jacobian[member][2] * rotation[2][column]
            for column in range(3)
        ]
        for member in range(2)
    ]
    whole = [
        [
            with_cam[member][0] * turn_q[0][column]
            + with_cam[member][1] * turn_q[1][column]
            + with_cam[member][2] * turn_q[2][column]
            for column in range(3)
        ]
        for member in range(2)
    ]
    cov_a = (
        squares[0] * whole[0][0] * whole[0][0]
        + squares[1] * whole[0][1] * whole[0][1]
        + squares[2] * whole[0][2] * whole[0][2]
        + 0.3
    )
    cov_b = (
        squares[0] * whole[0][0] * whole[1][0]
        + squares[1] * whole[0][1] * whole[1][1]
        + squares[2] * whole[0][2] * whole[1][2]
    )
    cov_c = (
        squares[0] * whole[1][0] * whole[1][0]
        + squares[1] * whole[1][1] * whole[1][1]
        + squares[2] * whole[1][2] * whole[1][2]
        + 0.3
    )
    determinant = cov_a * cov_c - cov_b * cov_b
    eye_pos = [
        -(
            rotation[0][column] * offset[0]
            + rotation[1][column] * offset[1]
            + rotation[2][column] * offset[2]
        )
        for column in range(3)
    ]
    heading = [centre_pos[column] - eye_pos[column] for column in range(3)]
    distance = jnp.sqrt(heading[0] * heading[0] + heading[1] * heading[1] + heading[2] * heading[2])
    basis = harmonics(heading[0] / distance, heading[1] / distance, heading[2] / distance)
    colours = [
        jnp.maximum(
            0.5
            + sum(
                (basis[number] * raw_params[:, 11 + 3 * number + channel] for number in range(16))
            ),
            0.0,
        )
        for channel in range(3)
    ]
    opacity = seen_mask / (1.0 + jnp.exp(-raw_params[:, 10]))
    return jnp.stack(
        [
            screen_x,
            screen_y,
            cov_c / determinant,
            -cov_b / determinant,
            cov_a / determinant,
            opacity,
        ]
        + colours,
        axis=1,
    )


def opacity_terms(features, across_x, across_y):
    dist_x = across_x[:, :, None] - features[:, 0][:, None, :]
    dist_y = across_y[:, :, None] - features[:, 1][:, None, :]
    exponent = (
        -0.5
        * (
            features[:, 2][:, None, :] * dist_x * dist_x
            + features[:, 4][:, None, :] * dist_y * dist_y
        )
        - features[:, 3][:, None, :] * dist_x * dist_y
    )
    alphas = features[:, 5][:, None, :] * jnp.exp(exponent)
    return (alphas, jnp.log1p(-alphas))


def before_sums(log_keep, upper):
    return jnp.einsum("tpg,gh->tph", log_keep, upper, precision=lax.Precision.HIGHEST)


def blend_slot(features, across_x, across_y, log_trans, colour, upper):
    alphas, log_keep = opacity_terms(features, across_x, across_y)
    weights = alphas * jnp.exp(log_trans[:, :, None] + before_sums(log_keep, upper))
    colour = colour + jnp.einsum(
        "tpg,tcg->tcp", weights, features[:, 6:9], precision=lax.Precision.HIGHEST
    )
    return (log_trans + jnp.sum(log_keep, axis=2), colour)


def request_lookup(codes, source_group, gauss_params, visible, cameras):
    blocks = gauss_params.shape[1] // GBLK
    is_live = codes >= 0
    clipped = jnp.maximum(codes, 0)
    local_slot = clipped % blocks
    view_ids = 2 * source_group + clipped // blocks
    raw_params = jnp.moveaxis(
        gauss_params.reshape(gauss_params.shape[0], blocks, GBLK)[:, local_slot], 0, 1
    )
    seen_mask = (
        visible.reshape(visible.shape[0], blocks, GBLK)[view_ids, local_slot].astype(jnp.float32)
        * is_live.astype(jnp.float32)[:, None]
    )
    chooser = (view_ids[:, None] == jnp.arange(cameras.shape[0], dtype=jnp.int32)[None, :]).astype(
        jnp.float32
    )
    camera = jnp.sum(chooser[:, :, None] * cameras[None, :, :], axis=1)
    return project(raw_params, camera, seen_mask)


def window_taps():
    offsets = jnp.arange(11).astype(jnp.float32) - 5.0
    taps = jnp.exp(-offsets * offsets / 4.5)
    return taps / jnp.sum(taps)


def blur(stack, row_count):
    taps = window_taps()
    columns = stack.shape[-1]
    widths = [(0, 0)] * (stack.ndim - 1) + [(5, 5)]
    wide = jnp.pad(stack, widths)
    across = sum((taps[number] * wide[..., number : number + columns] for number in range(11)))
    return sum((taps[number] * across[..., number : number + row_count, :] for number in range(11)))


def stripe_loss(images, targets, row_count):
    stack = jnp.stack([images, targets, images * images, targets * targets, images * targets])
    blurred = blur(stack, row_count)
    mean_x = blurred[0]
    mean_y = blurred[1]
    var_x = blurred[2] - mean_x * mean_x
    var_y = blurred[3] - mean_y * mean_y
    covar = blurred[4] - mean_x * mean_y
    ssim_map = (
        (2.0 * mean_x * mean_y + 0.0001)
        * (2.0 * covar + 0.0009)
        / ((mean_x * mean_x + mean_y * mean_y + 0.0001) * (var_x + var_y + 0.0009))
    )
    inner_x = images[..., 5 : 5 + row_count, :]
    inner_y = targets[..., 5 : 5 + row_count, :]
    return 0.8 * jnp.mean(jnp.abs(inner_x - inner_y), axis=-3) + 0.2 * (
        1.0 - jnp.mean(ssim_map, axis=-3)
    )


def local(gauss_params, visible, cameras, tile_ids, tile_blocks, target):
    cells = lax.axis_size("cell")
    groups = lax.axis_size("view")
    devices = cells * groups
    half = cells // 2
    quarter = cells // 4
    my_cell = lax.axis_index("cell")
    blocks = gauss_params.shape[1] // GBLK
    capacity = -(-blocks // devices)
    per_row = target.shape[3] // 16
    tile_list = tile_ids[0, 0]
    entries = tile_blocks[0, 0]
    tile_count, list_len = entries.shape
    stripe_no = tile_list // per_row
    column_no = tile_list % per_row
    shifted_no = (stripe_no - quarter) % cells
    anchor_x = 16 * column_no
    anchor_y = 16 * (shifted_no % half)
    view_side = shifted_no // half
    pixels = jnp.arange(256, dtype=jnp.int32)
    across_x = (anchor_x[:, None] + pixels[None, :] % 16).astype(jnp.float32)
    across_y = (anchor_y[:, None] + pixels[None, :] // 16).astype(jnp.float32)
    is_live = (entries >= 0).reshape(-1)
    keep_live = (entries >= 0).astype(jnp.float32)
    block_ids = jnp.maximum(entries, 0).reshape(-1)
    owner_flat = block_ids // blocks
    local_slot = block_ids % blocks
    serial = jnp.arange(tile_count * list_len, dtype=jnp.int32)
    earlier = (
        (owner_flat[:, None] == owner_flat[None, :])
        & is_live[None, :]
        & (serial[None, :] < serial[:, None])
    )
    rank_of = jnp.sum(earlier.astype(jnp.int32), axis=1)
    mailbox = owner_flat * capacity + rank_of
    send_box = jnp.where(is_live, mailbox, devices * capacity)
    read_box = jnp.where(is_live, mailbox, 0)
    request_codes = local_slot + blocks * jnp.repeat(view_side, list_len)
    asks = (
        jnp.full((devices * capacity,), -1, jnp.int32)
        .at[send_box]
        .set(request_codes, mode="drop")
        .reshape(cells, groups, capacity)
    )
    source_group = lax.broadcasted_iota(jnp.int32, (cells, groups, capacity), 1).reshape(-1)
    upper = (jnp.arange(GBLK)[:, None] < jnp.arange(GBLK)[None, :]).astype(jnp.float32)
    log_trans = jnp.zeros((tile_count, 256), jnp.float32)
    colour = jnp.zeros((tile_count, 3, 256), jnp.float32)
    incoming = lax.all_to_all(
        lax.all_to_all(asks, "cell", split_axis=0, concat_axis=0, tiled=True),
        "view",
        split_axis=1,
        concat_axis=1,
        tiled=True,
    )
    served = request_lookup(incoming.reshape(-1), source_group, gauss_params, visible, cameras)
    served = served.reshape(cells, groups, capacity, 9, GBLK)
    returned = lax.all_to_all(
        lax.all_to_all(served, "cell", split_axis=0, concat_axis=0, tiled=True),
        "view",
        split_axis=1,
        concat_axis=1,
        tiled=True,
    )
    lookup = returned.reshape(devices * capacity, 9, GBLK)[read_box].reshape(
        tile_count, list_len, 9, GBLK
    )
    for number in range(list_len):
        features = lookup[:, number]
        features = features.at[:, 5].multiply(keep_live[:, number][:, None])
        log_trans, colour = blend_slot(features, across_x, across_y, log_trans, colour, upper)
    spread = -(-tile_count // cells)
    serial_tiles = jnp.arange(tile_count, dtype=jnp.int32)
    same_stripe = (stripe_no[:, None] == stripe_no[None, :]) & (
        serial_tiles[None, :] < serial_tiles[:, None]
    )
    tile_rank = jnp.sum(same_stripe.astype(jnp.int32), axis=1)
    tile_box = stripe_no * spread + tile_rank
    out_pixels = (
        jnp.zeros((cells * spread, 3, 256), jnp.float32)
        .at[tile_box]
        .set(colour)
        .reshape(cells, spread, 3, 256)
    )
    out_columns = (
        jnp.full((cells * spread,), -1, jnp.int32)
        .at[tile_box]
        .set(column_no)
        .reshape(cells, spread)
    )
    got_pixels, got_columns = (
        lax.all_to_all(out_pixels, "cell", split_axis=0, concat_axis=0, tiled=True),
        lax.all_to_all(out_columns, "cell", split_axis=0, concat_axis=0, tiled=True),
    )
    flat_columns = got_columns.reshape(-1)
    place = jnp.where(flat_columns >= 0, flat_columns, per_row)
    stripe_tiles = (
        jnp.zeros((per_row, 3, 256), jnp.float32)
        .at[place]
        .set(got_pixels.reshape(-1, 3, 256), mode="drop")
    )
    stripe_image = (
        stripe_tiles.reshape(per_row, 3, 16, 16).transpose(1, 2, 0, 3).reshape(3, 16, per_row * 16)
    )
    both = jnp.stack([stripe_image, target[0]])
    padded = with_halo(both, (("cell", 2),), 5)
    row_pos = (my_cell - quarter) % cells % half
    row_index = jnp.arange(padded.shape[2], dtype=jnp.int32)
    keep_rows = ((row_index >= 5) | (row_pos != 0)) & ((row_index < 21) | (row_pos != half - 1))
    padded = padded * keep_rows.astype(jnp.float32)[None, None, :, None]
    loss_rows = stripe_loss(padded[0], padded[1], 16)
    return (stripe_image[None], loss_rows[None])


def solution(mesh):
    return jax.shard_map(
        local,
        mesh=mesh,
        in_specs=(
            P(None, ("cell", "view")),
            P(None, ("cell", "view")),
            P(),
            P("cell", "view", None),
            P("cell", "view", None, None),
            P("view", None, "cell", None),
        ),
        out_specs=(P("view", None, "cell", None), P("view", "cell", None)),
        check_vma=False,
    )
```

profile of v0, /device:TPU:0, one launch (start us, length us, event | category | flops | bytes accessed | tf_op | source)
XLA Modules:
  0.0 332.6 jit_solution(15135760724487018469)
XLA Ops:
  8.6 8.3 %all-to-all-start.1 = ((s32[16,2,5]{2,1,0:T(2,128)}), s32[16,2,5]{2,1,0:T(2,128)S(1)}, u32[]{:S(2)}, u32[]{:S(2)}) async-start(s32[16,2,5]{2,1,0:T(2,128)} %reshape.1510), calls=%async_computation.1 | async-start | bytes 32768 | tf_op jit(solution)/shard_map/all_to_all | solution.py:303
  17.9 5.2 %reshape.1511 = f32[59,150,128]{2,1,0:T(8,128)} reshape(f32[59,19200]{1,0:T(8,128)} %param.10) | data formatting | bytes 9062400 | tf_op jit(solution)/shard_map/reshape | solution.py:206
  23.1 5.4 %copy.110 = f32[59,150,128]{2,0,1:T(8,128)} copy(f32[59,150,128]{2,1,0:T(8,128)} %reshape.1511) | data formatting | bytes 9062400 | tf_op jit(solution)/shard_map/reshape | solution.py:206
  28.7 4.2 %all_to_all.34 = s32[16,2,5]{0,2,1:T(8,128)S(1)} all-to-all(s32[16,2,5]{0,2,1:T(8,128)S(1)} %copy.105), channel_id=1, replica_groups=mesh['cell'=16,'view'=2] {'view'}, dimensions={1} | all-to-all | bytes 1280 | tf_op jit(solution)/shard_map/all_to_all | solution.py:302
  35.3 5.6 %gather_fusion = f32[160,59,128]{2,1,0:T(8,128)} fusion(f32[59,150,128]{2,0,1:T(8,128)} %copy.110, s32[1024]{0:T(1024)S(1)} %pad_clamp_fusion.1), kind=kCustom, calls=%fused_computation | custom fusion | bytes 9667200 | tf_op jit(solution)/shard_map/gather | solution.py:206
  40.9 7.2 %fusion.104 = (f32[160,1,128]{2,1,0:T(1,128)S(1)}, f32[160,1,128]{2,1,0:T(1,128)S(1)}, f32[160,1,128]{2,1,0:T(1,128)S(1)}, f32[160,1,128]{2,1,0:T(1,128)S(1)}, f...) fusion(f32[160,59,128]{2,1,0:T(8,128)} %gather_fusion), kind=kLoop, calls=%fused_computation.284 | loop fusion | bytes 3112960 | tf_op jit(solution)/shard_map/slice | solution.py:150
  49.6 6.4 %fusion.103 = (f32[160,1,128]{2,1,0:T(1,128)S(1)}, f32[160,1,128]{2,1,0:T(1,128)S(1)}, f32[160,1,128]{2,1,0:T(1,128)S(1)}, f32[160,1,128]{2,1,0:T(1,128)S(1)}, f...) fusion(f32[160,59,128]{2,1,0:T(8,128)} %gather_fusion), kind=kLoop, calls=%fused_computation.283 | loop fusion | bytes 3112960 | tf_op jit(solution)/shard_map/slice | solution.py:150
  56.0 7.2 %fusion.102 = (f32[160,1,128]{2,1,0:T(1,128)S(1)}, f32[160,1,128]{2,1,0:T(1,128)}, f32[160,1,128]{2,1,0:T(1,128)}, f32[160,1,128]{2,1,0:T(1,128)}, f32[160,1,128...) fusion(f32[160,59,128]{2,1,0:T(8,128)} %gather_fusion), kind=kLoop, calls=%fused_computation.282 | loop fusion | bytes 3112960 | tf_op jit(solution)/shard_map/slice | solution.py:150
  65.9 2.0 multiply_add_fusion.5
  73.0 2.6 gather_fusion.1
  81.2 3.4 %stack.49 = f32[16,2,5,9,128]{4,3,2,1,0:T(8,128)S(1)} concatenate(f32[16,2,5,1,128]{4,3,2,1,0:T(1,128)} %bitcast.321, f32[16,2,5,1,128]{4,3,2,1,0:T(1,128)} %bitcast.322, f32[16,2,5,1,128]{4,3,2,1,0:T(1,128)S(1)} %bitcast.325, f32[16,2,5,1,128]{4,3,2,1,0:T(1,128)S(1)} %bitcast.324, f32[16,2,5,1,128]{4,3,2,1,0:T(1,128)} %bitcast.317, f32[16,2,5,1,128]{4,3,2,1,0:T(1,128)} %bitcast.326, ...), dimensions={3} | concatenate | bytes 1474560 | tf_op jit(solution)/shard_map/stack | solution.py:157
  85.8 6.9 %all-to-all-start.3 = ((f32[16,2,5,9,128]{4,1,3,2,0:T(2,128)}), f32[16,2,5,9,128]{4,1,3,2,0:T(2,128)S(1)}, u32[]{:S(2)}, u32[]{:S(2)}) async-start(f32[16,2,5,9,128]{4,1,3,2,0:T(2,128)} %copy.173), calls=%async_computation.3 | async-start | bytes 1474560 | tf_op jit(solution)/shard_map/all_to_all | solution.py:312
  98.1 13.8 %all-to-all-done.3 = f32[16,2,5,9,128]{4,1,3,2,0:T(2,128)S(1)} async-done(((f32[16,2,5,9,128]{4,1,3,2,0:T(2,128)}), f32[16,2,5,9,128]{4,1,3,2,0:T(2,128)S(1)}, u32[]{:S(2)}, u32[]{:S(2)}) %all-to-all-start.3) | async-done | bytes 737312 | tf_op jit(solution)/shard_map/all_to_all | solution.py:312
  112.0 4.3 %all_to_all.35 = f32[16,2,5,9,128]{4,0,3,2,1:T(8,128)S(1)} all-to-all(f32[16,2,5,9,128]{4,0,3,2,1:T(8,128)S(1)} %copy.174), channel_id=1, replica_groups=mesh['cell'=16,'view'=2] {'view'}, dimensions={1} | all-to-all | bytes 1474560 | tf_op jit(solution)/shard_map/all_to_all | solution.py:311
  116.3 4.9 %all-to-all-start = ((s32[16,1,8]{2,1,0:T(1,128)}), s32[16,1,8]{2,1,0:T(1,128)S(1)}, u32[]{:S(2)}, u32[]{:S(2)}) async-start(s32[16,1,8]{2,1,0:T(1,128)} %bitcast.7), calls=%async_computation | async-start | bytes 16384 | tf_op jit(solution)/shard_map/all_to_all | solution.py:346
  121.5 2.3 gather_fusion.2
  123.8 1.9 copy.177
  127.1 17.0 %fusion.20 = f32[120,256]{1,0:T(8,128)S(1)} fusion(f32[120,128]{1,0:T(8,128)S(1)} %bitcast.336, f32[120,128]{1,0:T(8,128)S(1)} %bitcast.339, f32[120,256]{1,0:T(8,128)S(1)} %get-tuple-element.190, f32[120,128]{1,0:T(8,128)S(1)} %bitcast.342, f32[120,128]{1,0:T(8,128)S(1)} %bitcast.345, f32[120,256]{1,0:T(8,128)S(1)} %get-tuple-element.191, ...), kind=kLoop, calls=%fused_computation.40 | loop fusion | flops 55019520 | bytes 737280 | tf_op jit(solution)/shard_map/reduce_sum | solution.py:196
  144.2 20.0 %fusion.21 = f32[120,256,128]{2,1,0:T(8,128)S(1)} fusion(f32[120,128]{1,0:T(8,128)S(1)} %bitcast.337, f32[120,128]{1,0:T(8,128)S(1)} %bitcast.340, f32[120,256]{1,0:T(8,128)S(1)} %get-tuple-element.190, f32[120,128]{1,0:T(8,128)S(1)} %bitcast.343, f32[120,128]{1,0:T(8,128)S(1)} %bitcast.346, f32[120,256]{1,0:T(8,128)S(1)} %get-tuple-element.191, ...), kind=kOutput, calls=%fused_computation.41 | convolution fusion | flops 6090932224 | bytes 16343040 | tf_op jit(solution)/shard_map/tpg,gh->tph/dot_general | solution.py:187
  164.6 20.2 %fusion.14 = f32[120,256,128]{2,1,0:T(8,128)S(1)} fusion(f32[120,128]{1,0:T(8,128)S(1)} %bitcast.350, f32[120,128]{1,0:T(8,128)S(1)} %bitcast.352, f32[120,128]{1,0:T(8,128)S(1)} %bitcast.354, f32[120,128]{1,0:T(8,128)S(1)} %bitcast.356, f32[120,128]{1,0:T(8,128)S(1)} %bitcast.348, f32[120,128]{1,0:T(8,128)S(1)} %broadcast_multiply_fusion, ...), kind=kOutput, calls=%fused_computation.33 | convolution fusion | flops 6090932224 | bytes 16343040 | tf_op jit(solution)/shard_map/tpg,gh->tph/dot_general | solution.py:187
  184.8 29.9 %fusion.10 = f32[120,3,256]{2,1,0:T(4,128)S(1)} fusion(f32[120,256,128]{2,1,0:T(8,128)S(1)} %fusion.14, f32[120,256]{1,0:T(8,128)S(1)} %fusion.20, f32[120,128]{1,0:T(8,128)S(1)} %bitcast.351, f32[120,128]{1,0:T(8,128)S(1)} %bitcast.353, f32[120,128]{1,0:T(8,128)S(1)} %bitcast.355, f32[120,128]{1,0:T(8,128)S(1)} %bitcast.357, f32[120,128]{1,0:T(8,128)S(1)} %bitcast.349, ...), kind=kOutput, calls=%fused_computation.29 | convolution fusion | flops 196608000 | bytes 17080320 | tf_op jit(solution)/shard_map/tpg,tcg->tcp/dot_general | solution.py:193
  214.8 25.4 %fusion.44 = f32[120,3,256]{2,1,0:T(4,128)S(1)} fusion(f32[120,3,256]{2,1,0:T(4,128)S(1)} %fusion.10, f32[120,256,128]{2,1,0:T(8,128)S(1)} %fusion.21, f32[120,128]{1,0:T(8,128)S(1)} %bitcast.338, f32[120,128]{1,0:T(8,128)S(1)} %bitcast.341, f32[120,256]{1,0:T(8,128)S(1)} %get-tuple-element.190, f32[120,128]{1,0:T(8,128)S(1)} %bitcast.344, ...), kind=kOutput, calls=%fused_computation.78 | convolution fusion | flops 192768000 | bytes 17448960 | tf_op jit(solution)/shard_map/tpg,tcg->tcp/dot_general | solution.py:193
  240.2 4.4 %scatter_fusion = f32[128,3,256]{2,1,0:T(4,128)S(1)} fusion(f32[128,3,256]{2,1,0:T(4,128)S(1)} %broadcast_in_dim.21, s32[120]{0:T(128)S(1)} %fusion.87, f32[120,3,256]{2,1,0:T(4,128)S(1)} %fusion.44), kind=kCustom, calls=%fused_computation.5 | custom fusion | bytes 1106400 | tf_op jit(solution)/shard_map/scatter | solution.py:335
  245.4 7.0 %all-to-all-start.5 = ((f32[16,8,3,256]{3,1,2,0:T(8,128)}), f32[16,8,3,256]{3,1,2,0:T(8,128)S(1)}, u32[]{:S(2)}, u32[]{:S(2)}) async-start(f32[16,8,3,256]{3,1,2,0:T(8,128)} %copy.181), calls=%async_computation.5 | async-start | bytes 786432 | tf_op jit(solution)/shard_map/all_to_all | solution.py:345
  254.4 10.4 %all-to-all-done.5 = f32[16,8,3,256]{3,1,2,0:T(8,128)S(1)} async-done(((f32[16,8,3,256]{3,1,2,0:T(8,128)}), f32[16,8,3,256]{3,1,2,0:T(8,128)S(1)}, u32[]{:S(2)}, u32[]{:S(2)}) %all-to-all-start.5) | async-done | bytes 393248 | tf_op jit(solution)/shard_map/all_to_all | solution.py:345
  265.2 4.3 %scatter_fusion.1 = f32[120,3,256]{2,1,0:T(4,128)S(1)} fusion(f32[120,3,256]{2,1,0:T(4,128)S(1)} %broadcast_in_dim.18, s32[128]{0:T(128)S(1)} %fusion.88, f32[128,3,256]{2,1,0:T(4,128)S(1)} %copy.183), kind=kCustom, calls=%fused_computation.6 | custom fusion | bytes 1180160 | tf_op jit(solution)/shard_map/scatter | solution.py:353
  270.5 1.9 copy.185
  275.9 2.3 collective-permute-start.1
  279.6 7.6 %collective-permute-done.1 = f32[2,3,5,1920]{3,2,1,0:T(8,128)S(1)} collective-permute-done((f32[2,3,5,1920]{3,2,1,0:T(8,128)S(1)}, f32[2,3,5,1920]{3,2,1,0:T(8,128)S(1)}, u32[]{:S(2)}, u32[]{:S(2)}) %collective-permute-start.1) | collective-permute-done | bytes 230432 | tf_op jit(solution)/shard_map/ppermute | solution.py:18
  287.3 4.0 %collective-permute-done = f32[2,3,5,1920]{3,2,1,0:T(8,128)S(1)} collective-permute-done((f32[2,3,5,1920]{3,2,1,0:T(8,128)S(1)}, f32[2,3,5,1920]{3,2,1,0:T(8,128)S(1)}, u32[]{:S(2)}, u32[]{:S(2)}) %collective-permute-start) | collective-permute-done | bytes 230432 | tf_op jit(solution)/shard_map/ppermute | solution.py:16
  292.9 17.9 %multiply_add_fusion = f32[5,3,26,1920]{3,2,1,0:T(8,128)} fusion(f32[5,3,26,1920]{3,2,1,0:T(8,128)S(1)} %pad_maximum_fusion, f32[]{:T(128)} %bitcast.80, f32[]{:T(128)} %bitcast.79, f32[]{:T(128)} %bitcast.78, f32[]{:T(128)} %bitcast.77, f32[]{:T(128)} %bitcast.76, f32[]{:T(128)} %bitcast.75, f32[]{:T(128)} %bitcast.74, f32[]{:T(128)} %bitcast.73, ...), kind=kLoop, calls=%fused_computation.44 | loop fusion | flops 15724800 | bytes 5990444 | tf_op jit(solution)/shard_map/add | solution.py:230
  310.8 19.4 %fusion.34 = f32[5,3,16,1920]{3,2,1,0:T(8,128)S(1)} fusion(f32[5,3,26,1920]{3,2,1,0:T(8,128)} %multiply_add_fusion, f32[]{:T(128)} %bitcast.80, f32[]{:T(128)} %bitcast.79, f32[]{:T(128)} %bitcast.78, f32[]{:T(128)} %bitcast.77, f32[]{:T(128)} %bitcast.76, f32[]{:T(128)} %bitcast.75, f32[]{:T(128)} %bitcast.74, f32[]{:T(128)} %bitcast.73, f32[]{:T(128)} %bitcast.72, ...), kind=kLoop, calls=%fused_computation.57 | loop fusion | flops 9676800 | bytes 22118444 | tf_op jit(solution)/shard_map/add | solution.py:231
  (116 shorter events, 48.0 us)
Async XLA Ops:
  0.6 72.3 %copy-start = (s32[4,19200]{1,0:T(4,128)S(1)}, s32[4,19200]{1,0:T(4,128)}, u32[]{:S(2)}) copy-start(s32[4,19200]{1,0:T(4,128)} %param.11) | copy-start | bytes 921604
  8.6 20.0 %all-to-all-start.1 = ((s32[16,2,5]{2,1,0:T(2,128)}), s32[16,2,5]{2,1,0:T(2,128)S(1)}, u32[]{:S(2)}, u32[]{:S(2)}) async-start(s32[16,2,5]{2,1,0:T(2,128)} %reshape.1510), calls=%async_computation.1 | async-start | bytes 32768 | tf_op jit(solution)/shard_map/all_to_all | solution.py:303
  34.1 30.2 %copy-start.2 = (f32[160,1]{0,1:T(1,128)}, f32[160,1]{0,1:T(1,128)S(1)}, u32[]{:S(2)}) copy-start(f32[160,1]{0,1:T(1,128)S(1)} %get-tuple-element.163) | copy-start | bytes 1924
  85.8 26.1 %all-to-all-start.3 = ((f32[16,2,5,9,128]{4,1,3,2,0:T(2,128)}), f32[16,2,5,9,128]{4,1,3,2,0:T(2,128)S(1)}, u32[]{:S(2)}, u32[]{:S(2)}) async-start(f32[16,2,5,9,128]{4,1,3,2,0:T(2,128)} %copy.173), calls=%async_computation.3 | async-start | bytes 1474560 | tf_op jit(solution)/shard_map/all_to_all | solution.py:312
  116.3 129.1 %all-to-all-start = ((s32[16,1,8]{2,1,0:T(1,128)}), s32[16,1,8]{2,1,0:T(1,128)S(1)}, u32[]{:S(2)}, u32[]{:S(2)}) async-start(s32[16,1,8]{2,1,0:T(1,128)} %bitcast.7), calls=%async_computation | async-start | bytes 16384 | tf_op jit(solution)/shard_map/all_to_all | solution.py:346
  245.4 19.4 %all-to-all-start.5 = ((f32[16,8,3,256]{3,1,2,0:T(8,128)}), f32[16,8,3,256]{3,1,2,0:T(8,128)S(1)}, u32[]{:S(2)}, u32[]{:S(2)}) async-start(f32[16,8,3,256]{3,1,2,0:T(8,128)} %copy.181), calls=%async_computation.5 | async-start | bytes 786432 | tf_op jit(solution)/shard_map/all_to_all | solution.py:345
  275.9 11.3 %collective-permute-start.1 = (f32[2,3,5,1920]{3,2,1,0:T(8,128)S(1)}, f32[2,3,5,1920]{3,2,1,0:T(8,128)S(1)}, u32[]{:S(2)}, u32[]{:S(2)}) collective-permute-start(f32[2,3,5,1920]{3,2,1,0:T(8,128)S(1)} %get-tuple-element.137), channel_id=1, source_target_pairs={{2,0},{4,2},{6,4},{8,6},{10,8},{12,10},{14,12},{16,14},{18,16},{20... | collective-permute-start | bytes 691208 | tf_op jit(solution)/shard_map/ppermute | solution.py:18
  278.2 13.0 %collective-permute-start = (f32[2,3,5,1920]{3,2,1,0:T(8,128)S(1)}, f32[2,3,5,1920]{3,2,1,0:T(8,128)S(1)}, u32[]{:S(2)}, u32[]{:S(2)}) collective-permute-start(f32[2,3,5,1920]{3,2,1,0:T(8,128)S(1)} %get-tuple-element.136), channel_id=1, source_target_pairs={{0,2},{2,4},{4,6},{6,8},{8,10},{10,12},{12,14},{14,16},{16,18},{18... | collective-permute-start | bytes 691208 | tf_op jit(solution)/shard_map/ppermute | solution.py:16
  292.9 39.4 %copy-start.1 = (s32[4,19200]{1,0:T(4,128)S(1)}, s32[4,19200]{1,0:T(4,128)}, u32[]{:S(2)}) copy-start(s32[4,19200]{1,0:T(4,128)} %param.11) | copy-start | bytes 921604
where the time goes:
time: 338 us; the launch traced here: 333 us
  matrix products  95.4 us (28%)
  other arithmetic  83.1 us (25%)
  local copies, waits for them, and re-layouts  78.9 us (23%)
  waiting for transfers between devices  35.9 us (11%)
  starting transfers between devices  29.4 us (9%)
  blocking collectives  8.51 us (3%)
    dot_general x2, matrix products, blend_slot(): jnp.einsum('tpg,tcg->tcp', weights, features[:, 6:9], precision=lax.Preci...  55.3 us
    dot_general x2, matrix products, before_sums(): jnp.einsum('tpg,gh->tph', log_keep, upper, precision=lax.Precision.HIGHEST)  40.2 us
    slice x3, local copies, waits for them, and re-layouts, project(): raw_params[:, 11 + 3 * number + channel]  20.8 us
    add x1, other arithmetic, blur(): sum((taps[number] * across[..., number:number + row_count, :] for number...  19.4 us
    add x1, other arithmetic, blur(): sum((taps[number] * wide[..., number:number + columns] for number in rang...  17.9 us
    reduce_sum x1, other arithmetic, blend_slot(): return (log_trans + jnp.sum(log_keep, axis=2), colour)  17 us
    all_to_all x1, waiting for transfers between devices, local(): lax.all_to_all(served, 'cell', split_axis=0, concat_axis=0, tiled=True)  13.8 us
    reshape x2, local copies, waits for them, and re-layouts, request_lookup(): gauss_params.reshape(gauss_params.shape[0], blocks, GBLK)[:, local_slot]  10.7 us
  transfers between devices with their start and end apart: 6, of which 4 were waited for; matrix products, arithmetic and copies ran while one was open for 43% of the time, Pallas kernels for 0%

commit v1 on v0

v1 whole, which is shorter than its diff:
```python
import functools
import math

import jax
import jax.numpy as jnp
from jax import lax
from jax.experimental import pallas as pl
from jax.experimental.pallas import tpu as pltpu
from jax.sharding import PartitionSpec as P

GBLK = 128
LANES = 128
LOG2E = math.log2(math.e)
VMEM = pltpu.VMEM
SMEM = pltpu.SMEM
F32 = jnp.float32


def iota(shape, dim):
    return lax.broadcasted_iota(jnp.int32, shape, dim)


def split(value, size):
    whole = jnp.floor((value + 0.5) * (1.0 / size))
    return whole, value - whole * size


def own_route(cells, groups, blocks, cap, rcap, per_row, ids_ref, lists_ref, route_ref, box):
    length, tiles = lists_ref.shape
    box[...] = jnp.full(box.shape, -1.0, F32)
    box[0:length, 0:tiles] = lists_ref[...].astype(F32)
    box[length : length + 1, 0:tiles] = ids_ref[...].astype(F32)
    rows = box[...]
    columns = rows.T
    earlier = iota((LANES, LANES), 1) < iota((LANES, LANES), 0)

    def count(mask):
        return jnp.sum(jnp.where(mask, 1.0, 0.0), axis=1, keepdims=True)

    stripe, _ = split(columns[:, length : length + 1], per_row)
    stripe_row, _ = split(rows[length : length + 1, :], per_row)
    tile_rank = count((stripe == stripe_row) & earlier)
    owner_rows = [split(rows[n : n + 1, :], blocks)[0] for n in range(length)]
    values = []
    for n in range(length):
        entry = columns[:, n : n + 1]
        owner, _ = split(entry, blocks)
        rank = count((owner == owner_rows[n]) & earlier)
        for m in range(n):
            rank = rank + count(owner == owner_rows[m])
        values.append(jnp.where(entry >= 0.0, owner * cap + rank, -1.0))
    values.append(stripe * rcap + tile_rank)
    lane = iota((LANES, LANES), 1)
    route = jnp.zeros((LANES, LANES), F32)
    for number, value in enumerate(values):
        route = jnp.where(lane == number, value, route)
    route_ref[...] = route.T[0:8, :].astype(jnp.int32)


def harmonics(x, y, z):
    xx, yy, zz = x * x, y * y, z * z
    return [
        None,
        -0.4886025119029199 * y,
        0.4886025119029199 * z,
        -0.4886025119029199 * x,
        1.0925484305920792 * x * y,
        -1.0925484305920792 * y * z,
        0.31539156525252005 * (2.0 * zz - xx - yy),
        -1.0925484305920792 * x * z,
        0.5462742152960396 * (xx - yy),
        -0.5900435899266435 * y * (3.0 * xx - yy),
        2.890611442640554 * x * y * z,
        -0.4570457994644658 * y * (4.0 * zz - xx - yy),
        0.3731763325901154 * z * (2.0 * zz - 3.0 * xx - 3.0 * yy),
        -0.4570457994644658 * x * (4.0 * zz - xx - yy),
        1.445305721320277 * z * (xx - yy),
        -0.5900435899266435 * x * (xx - 3.0 * yy),
    ]


def view_free(param):
    mean = [param(n) for n in range(3)]
    re, qx, qy, qz = [param(6 + n) for n in range(4)]
    inv_sq = 2.0 / (re * re + qx * qx + qy * qy + qz * qz)
    sqx, sqy, sqz = qx * inv_sq, qy * inv_sq, qz * inv_sq
    xx, yy, zz = qx * sqx, qy * sqy, qz * sqz
    xy, xz, yz = qx * sqy, qx * sqz, qy * sqz
    rx, ry, rz = re * sqx, re * sqy, re * sqz
    turn = [
        [1.0 - (yy + zz), xy - rz, xz + ry],
        [xy + rz, 1.0 - (xx + zz), yz - rx],
        [xz - ry, yz + rx, 1.0 - (xx + yy)],
    ]
    scale = [jnp.exp(2.0 * param(3 + n)) for n in range(3)]
    log_opacity = -LOG2E * jnp.log(1.0 + jnp.exp(-param(10)))
    return mean, turn, scale, log_opacity


def project(param, free, cam, seen):
    mean, turn, scale, log_opacity = free
    rot = [[cam(3 * i + j) for j in range(3)] for i in range(3)]
    shift = [cam(9 + i) for i in range(3)]
    focal = cam(12)
    pc = [rot[i][0] * mean[0] + rot[i][1] * mean[1] + rot[i][2] * mean[2] + shift[i] for i in range(3)]
    inv_depth = 1.0 / pc[2]
    scaled = focal * inv_depth
    off_x = scaled * pc[0]
    off_y = scaled * pc[1]
    jac_x = off_x * inv_depth
    jac_y = off_y * inv_depth
    with_cam = [
        [scaled * rot[0][j] - jac_x * rot[2][j] for j in range(3)],
        [scaled * rot[1][j] - jac_y * rot[2][j] for j in range(3)],
    ]
    whole = [
        [sum(with_cam[i][m] * turn[m][j] for m in range(3)) for j in range(3)] for i in range(2)
    ]
    heavy = [[scale[j] * whole[i][j] for j in range(3)] for i in range(2)]
    cov_a = heavy[0][0] * whole[0][0] + heavy[0][1] * whole[0][1] + heavy[0][2] * whole[0][2] + 0.3
    cov_b = heavy[0][0] * whole[1][0] + heavy[0][1] * whole[1][1] + heavy[0][2] * whole[1][2]
    cov_c = heavy[1][0] * whole[1][0] + heavy[1][1] * whole[1][1] + heavy[1][2] * whole[1][2] + 0.3
    inv_det = LOG2E / (cov_a * cov_c - cov_b * cov_b)
    eye = [rot[0][j] * shift[0] + rot[1][j] * shift[1] + rot[2][j] * shift[2] for j in range(3)]
    head = [mean[j] + eye[j] for j in range(3)]
    inv_dist = lax.rsqrt(head[0] * head[0] + head[1] * head[1] + head[2] * head[2])
    basis = harmonics(*[part * inv_dist for part in head])
    colours = []
    for channel in range(3):
        total = 0.5 + 0.28209479177387814 * param(11 + channel)
        for j in range(1, 16):
            total = total + basis[j] * param(11 + 3 * j + channel)
        colours.append(jnp.maximum(total, 0.0))
    return [
        off_x + cam(13),
        off_y + cam(14),
        -0.5 * cov_c * inv_det,
        cov_b * inv_det,
        -0.5 * cov_a * inv_det,
        jnp.where(seen > 0, log_opacity, -1e30),
    ] + colours


def prepare_kernel(
    cells, groups, cap, rcap, per_row,
    cams_ref, ids_ref, lists_ref, params_ref, seen_ref, feats_ref, route_ref, box, stage, seen_stage,
):
    features, total = params_ref.shape
    blocks = total // GBLK
    views = seen_ref.shape[0]
    own_route(cells, groups, blocks, cap, rcap, per_row, ids_ref, lists_ref, route_ref, box)

    @pl.loop(0, -(-blocks // 8))
    def _(group):
        first = jnp.minimum(8 * group, blocks - 8)
        for b in range(8):
            lanes = pl.ds(pl.multiple_of((first + b) * GBLK, GBLK), GBLK)
            for i in range(-(-features // 8)):
                high = min(8, features - 8 * i)
                stage[pl.ds((8 * i + b) * 8, high), :] = params_ref[pl.ds(8 * i, high), lanes]
            seen_stage[pl.ds(8 * b, views), :] = seen_ref[:, lanes]

        def param(r):
            return stage[pl.ds((r // 8) * 64 + r % 8, 8, stride=8), :]

        free = view_free(param)
        for view in range(views):
            seen = seen_stage[pl.ds(view, 8, stride=8), :]
            made = project(param, free, lambda number: cams_ref[view, number], seen)
            for number, value in enumerate(made):
                feats_ref[view, number, pl.ds(first, 8), :] = value


def render_kernel(
    cells, groups, cap, rcap, per_row, blocks,
    me_ref, table_ref, feats_ref, early_up, early_down, out_ref, code_ref,
    box, info, turned, shades, rest, sheets, code_box, code_smem, sem,
):
    del early_up, early_down
    devices = cells * groups
    quarter, half = cells // 4, cells // 2
    length, tiles = table_ref.shape[1] - 1, table_ref.shape[2]
    views = feats_ref.shape[0]
    box[...] = jnp.full(box.shape, -1.0, F32)
    for n in range(length + 1):
        box[n, :, 0:tiles] = table_ref[:, n, :].astype(F32)
    me = me_ref[0].astype(F32)
    my_stripe = me_ref[1].astype(F32)
    before = jnp.where(iota((LANES, LANES), 0) < iota((LANES, LANES), 1), 1.0, 0.0)

    def ranks(mask):
        ones = jnp.where(mask, 1.0, 0.0)
        return jnp.dot(ones, before, preferred_element_type=F32), jnp.sum(ones, axis=1, keepdims=True)

    def pick(mask, value):
        return jnp.sum(jnp.where(mask, value, 0.0), axis=1, keepdims=True)

    stripe, column = split(box[length], per_row)
    shifted = stripe - quarter
    shifted = jnp.where(shifted < 0.0, shifted + cells, shifted)
    group_of = jnp.bitwise_and(iota((devices, 1), 0), groups - 1).astype(F32)
    tile_code = column + 128.0 * shifted + 16384.0 * group_of
    code_lane = iota((devices, LANES), 1)
    codes = jnp.zeros((devices, LANES), F32)
    prior = jnp.zeros((devices, 1), F32)
    mine = []
    for n in range(length):
        owner, local_slot = split(box[n], blocks)
        hit = owner == me
        rank, total = ranks(hit)
        mine.append((hit, rank + prior, local_slot))
        prior = prior + total
    slot_lane = iota((devices, 2 * LANES), 1).astype(F32)
    found = jnp.zeros((1, 2 * LANES), F32)
    for k in range(cap):
        asked = sum(pick(hit & (rank == k), local_slot + 1.0) for hit, rank, local_slot in mine)
        tile = sum(pick(hit & (rank == k), tile_code) for hit, rank, local_slot in mine)
        codes = jnp.where(code_lane == k, asked, codes)
        found = found + jnp.sum(jnp.where(slot_lane == asked - 1.0, tile, 0.0), axis=0, keepdims=True)
    here = stripe == my_stripe
    rank, _ = ranks(here)
    for k in range(rcap):
        codes = jnp.where(code_lane == cap + k, pick(here & (rank == k), column + 1.0), codes)
    code_box[...] = codes.astype(jnp.int32)
    code_ref[...] = codes.astype(jnp.int32)
    scalars = pltpu.make_async_copy(code_box, code_smem, sem)
    scalars.start()

    for part in range(2):
        row = found[:, part * LANES : (part + 1) * LANES]
        info[pl.ds(part * LANES, LANES), :] = jnp.broadcast_to(row, (LANES, LANES)).T
    for part in range(2):
        count = (LANES, 32)[part]
        rows = pl.ds(part * LANES, count)
        tile = info[rows, :].astype(jnp.int32)
        column = jnp.bitwise_and(tile, 127)
        shifted = jnp.bitwise_and(tile >> 7, 127)
        side = (shifted >= half).astype(jnp.int32)
        view = 2 * (tile >> 14) + side
        anchors = [(16 * column).astype(F32), (16 * (shifted - side * half)).astype(F32)]
        is_view = [view == w for w in range(1, views)]
        for number in range(9):
            value = feats_ref[0, number, rows, :]
            for w in range(1, views):
                value = jnp.where(is_view[w - 1], feats_ref[w, number, rows, :], value)
            if number < 2:
                value = value - anchors[number]
            if part == 1:
                value = jnp.concatenate([value] * 4, axis=0)
            turned[part, number] = value.T

    across = [iota((8, LANES), 0).astype(F32) + 8.0 * xh for xh in range(2)]
    unroll = 4

    def composite(part, pixel_rows):
        def steps(n, carry):
            trans = list(carry[0])
            colour = [list(rows) for rows in carry[1]]
            for u in range(unroll):
                sx, sy, ca, cb, cc, lo, *shade = [
                    jnp.broadcast_to(turned[part, f, pl.ds(unroll * n + u, 1), :], (8, LANES))
                    for f in range(9)
                ]
                dx = [across[xh] - sx for xh in range(2)]
                flat = [ca * dx[xh] * dx[xh] + lo for xh in range(2)]
                mixed = [cb * dx[xh] for xh in range(2)]
                for yl in range(4):
                    dy = pixel_rows[yl] - sy
                    bend = cc * dy
                    for xh in range(2):
                        v = 2 * yl + xh
                        weight = jnp.exp2(flat[xh] + dy * (mixed[xh] + bend)) * trans[v]
                        trans[v] = trans[v] - weight
                        for c in range(3):
                            colour[c][v] = colour[c][v] + weight * shade[c]
            return tuple(trans), tuple(tuple(rows) for rows in colour)

        zero = jnp.zeros((8, LANES), F32)
        start = (tuple(zero + 1.0 for _ in range(8)), tuple(tuple(zero for _ in range(8)) for _ in range(3)))
        trans, colour = lax.fori_loop(0, GBLK // unroll, steps, start)
        return [*colour, trans]

    @pl.loop(0, 4)
    def _(chunk):
        high, odd = chunk >> 1, jnp.bitwise_and(chunk, 1)
        pixel_rows = [
            (8 * high + jnp.bitwise_and(8 - 4 * odd - yl, 7)).astype(F32) for yl in range(4)
        ]
        planes = composite(0, pixel_rows)
        for c in range(4):
            for v in range(8):
                shades[pl.ds(c * 256 + chunk * 64 + 8 * v, 8), :] = planes[c][v]

    chunk = iota((8, LANES), 1) >> 5
    high, odd = chunk >> 1, jnp.bitwise_and(chunk, 1)
    pixel_rows = [
        (8 * high + jnp.bitwise_and(8 - 4 * odd - yl, 7)).astype(F32) for yl in range(4)
    ]
    planes = composite(1, pixel_rows)
    for c in range(4):
        for v in range(8):
            rest[pl.ds(c * 64 + 8 * v, 8), :] = planes[c][v]

    for r in range(8):
        sheets[pl.ds(r, LANES, stride=8), :] = shades[pl.ds(r * LANES, LANES), :].T
    left = iota((32, LANES), 1) < 64
    for pair in range(2):
        both = rest[pl.ds(pair * LANES, LANES), :].T
        parts = [both[32 * q : 32 * q + 32, :] for q in range(4)]
        swapped = [pltpu.roll(part, 64, 1) for part in parts]
        for h in range(2):
            low = jnp.where(left, parts[2 * h], swapped[2 * h + 1])
            high = jnp.where(left, swapped[2 * h], parts[2 * h + 1])
            sheets[pl.ds(LANES * 8 + 4 * pair + h, 32, stride=8), :] = low
            sheets[pl.ds(LANES * 8 + 4 * pair + 2 + h, 32, stride=8), :] = high
    scalars.wait()

    @pl.loop(0, devices)
    def _(d):
        for k in range(cap):
            place = jnp.clip(code_smem[d, k] - 1, 0, blocks - 1)
            out_ref[d, pl.ds(8 * k, 8), :] = sheets[pl.ds(pl.multiple_of(8 * place, 8), 8), :]


def combine_kernel(tiles, route_ref, got_ref, fixed_ref, out_ref):
    del fixed_ref
    line = iota((8, LANES), 0)

    @pl.loop(0, tiles, unroll=8)
    def _(t):
        front = route_ref[0, t]
        back = route_ref[1, t]
        where_to = route_ref[2, t]
        near = got_ref[pl.ds(pl.multiple_of(8 * front, 8), 8), :]
        far = got_ref[pl.ds(pl.multiple_of(8 * jnp.maximum(back, 0), 8), 8), :]
        keep = jnp.where(line >= 6, near, 0.0)
        keep = keep + pltpu.roll(keep, 4, 0)
        keep = keep + pltpu.roll(keep, 2, 0)
        tile = near + jnp.where(back >= 0, keep * far, 0.0)
        out_ref[pl.ds(6 * where_to, 6), :] = tile[0:6, :]


def place_kernel(
    groups, cap, rcap, per_row, code_ref, me_ref, got_ref, image_ref, head_ref, tail_ref, board
):
    cells = got_ref.shape[0]

    @pl.loop(0, cells)
    def _(cell):
        for k in range(rcap):
            column = code_ref[cell * groups + me_ref[2], cap + k] - 1
            spot = jnp.where(column < 0, per_row, column)
            board[pl.ds(8 * spot, 6), :] = got_ref[cell, 6 * k : 6 * k + 6, :]

    group = iota((8, LANES), 1) >> 4
    masks = [jnp.bitwise_and(group, bit) != 0 for bit in (1, 2, 4)]
    for j in range(per_row // 8):
        for c in range(3):
            for h in range(2):
                made = board[pl.ds(64 * j + 2 * c + h, 8, stride=8), :]
                made = pltpu.roll(made, 0, 1, stride=16, stride_axis=0)
                for mask, bit in zip(masks, (1, 2, 4)):
                    made = jnp.where(mask, pltpu.roll(made, 8 - bit, 0), made)
                made = pltpu.roll(made, 0, 1, stride=16, stride_axis=0)
                image_ref[0, c, 8 * h : 8 * h + 8, 128 * j : 128 * j + 128] = made
    head_ref[...] = image_ref[0, :, 0:5, :]
    tail_ref[...] = image_ref[0, :, 11:16, :]


def window_taps():
    raw = [math.exp(-k * k / 4.5) for k in range(6)]
    whole = raw[0] + 2.0 * sum(raw[1:])
    return [value / whole for value in raw]


def across_rows(tall, first, count):
    taps = window_taps()
    around = (count + 2) * LANES
    blurred = []
    for f in range(tall.shape[0]):
        given = tall[f, :, LANES * first : LANES * first + around]
        total = taps[0] * given
        for k in range(1, 6):
            total = total + taps[k] * (pltpu.roll(given, k, 1) + pltpu.roll(given, around - k, 1))
        blurred.append(total[:, LANES : LANES + count * LANES])
    return blurred


def clear_sides(tall):
    blank = jnp.zeros((tall.shape[0], 16, LANES), F32)
    tall[:, :, 0:LANES] = blank
    tall[:, :, tall.shape[2] - LANES :] = blank


def down_columns(fields, f):
    taps = window_taps()
    total = taps[0] * fields[f, 5:21, :]
    for k in range(1, 6):
        total = total + taps[k] * (fields[f, 5 - k : 21 - k, :] + fields[f, 5 + k : 21 + k, :])
    return total


def span(j):
    return pl.ds(pl.multiple_of(LANES * j, LANES), LANES)


RUN = 5


def target_kernel(target_ref, up_ref, down_ref, late_ref, out_ref, fields, tall):
    del late_ref
    spans = target_ref.shape[3] // LANES
    clear_sides(tall)

    @pl.loop(0, 3)
    def _(c):
        @pl.loop(0, spans)
        def _(j):
            fields[0, 0:5, :] = up_ref[c, :, span(j)]
            fields[0, 5:21, :] = target_ref[0, c, :, span(j)]
            fields[0, 21:26, :] = down_ref[c, :, span(j)]
            fields[1] = fields[0] * fields[0]
            for f in range(2):
                tall[f, :, span(j + 1)] = down_columns(fields, f)

        for first in range(0, spans, RUN):
            count = min(RUN, spans - first)
            for f, value in enumerate(across_rows(tall, first, count)):
                out_ref[f, c, :, LANES * first : LANES * (first + count)] = value


def own_kernel(image_ref, target_ref, out_ref, fields, tall):
    spans = target_ref.shape[3] // LANES
    clear_sides(tall)
    fields[...] = jnp.zeros(fields.shape, F32)

    @pl.loop(0, 3)
    def _(c):
        @pl.loop(0, spans)
        def _(j):
            x = image_ref[0, c, :, span(j)]
            y = target_ref[0, c, :, span(j)]
            fields[0, 5:21, :] = x
            fields[1, 5:21, :] = x * x
            fields[2, 5:21, :] = x * y
            for f in range(3):
                tall[f, :, span(j + 1)] = down_columns(fields, f)

        for first in range(0, spans, RUN):
            count = min(RUN, spans - first)
            for f, value in enumerate(across_rows(tall, first, count)):
                out_ref[f, c, :, LANES * first : LANES * (first + count)] = value


def loss_kernel(
    image_ref, target_ref, own_ref, fixed_ref, up_ref, down_ref, target_up, target_down,
    image_out, loss_ref, fields, tall,
):
    taps = window_taps()
    image_out[...] = image_ref[...]
    spans = image_ref.shape[3] // LANES
    clear_sides(tall)
    fields[...] = jnp.zeros(fields.shape, F32)

    @pl.loop(0, 3)
    def _(c):
        @pl.loop(0, spans)
        def _(j):
            x = up_ref[c, :, span(j)]
            y = target_up[c, :, span(j)]
            for f, value in enumerate((x, x * x, x * y)):
                fields[f, 3:8, :] = value
            x = down_ref[c, :, span(j)]
            y = target_down[c, :, span(j)]
            for f, value in enumerate((x, x * x, x * y)):
                fields[f, 24:29, :] = value
            for f in range(3):
                above = taps[1] * fields[f, 7:15, :]
                below = taps[1] * fields[f, 17:25, :]
                for k in range(2, 6):
                    above = above + taps[k] * fields[f, 8 - k : 16 - k, :]
                    below = below + taps[k] * fields[f, 16 + k : 24 + k, :]
                tall[f, 0:8, span(j + 1)] = above
                tall[f, 8:16, span(j + 1)] = below

        for first in range(0, spans, RUN):
            count = min(RUN, spans - first)
            lanes = slice(LANES * first, LANES * (first + count))
            mx, xx, xy = [
                value + own_ref[f, c, :, lanes]
                for f, value in enumerate(across_rows(tall, first, count))
            ]
            my = fixed_ref[0, c, :, lanes]
            both = mx * my
            sums = mx * mx + my * my
            ssim = (2.0 * both + 0.0001) * (2.0 * (xy - both) + 0.0009) / (
                (sums + 0.0001) * (xx + fixed_ref[1, c, :, lanes] - sums + 0.0009)
            )
            gap = jnp.abs(image_ref[0, c, :, lanes] - target_ref[0, c, :, lanes])
            part = (0.8 / 3.0) * gap - (0.2 / 3.0) * ssim
            loss_ref[0, :, lanes] = jnp.where(c == 0, 0.2, loss_ref[0, :, lanes]) + part


def call(kernel, outs, specs, scratch=(), mem=16, work=0):
    return pl.pallas_call(
        kernel,
        out_shape=outs,
        in_specs=[pl.BlockSpec(memory_space=spec) for spec in specs],
        scratch_shapes=list(scratch),
        cost_estimate=pl.CostEstimate(flops=work, bytes_accessed=0, transcendentals=0) if work else None,
        compiler_params=pltpu.CompilerParams(vmem_limit_bytes=mem * 2**20),
    )


def local(gauss_params, visible, cameras, tile_ids, tile_blocks, target):
    cells = lax.axis_size("cell")
    groups = lax.axis_size("view")
    devices = cells * groups
    half = cells // 2
    quarter = cells // 4
    blocks = gauss_params.shape[1] // GBLK
    cap = -(-blocks // devices)
    width = target.shape[3]
    per_row = width // 16
    tiles = tile_ids.shape[2]
    rcap = -(-tiles // cells)
    length = tile_blocks.shape[3]
    rows = LANES + 32
    shape = jax.ShapeDtypeStruct
    my_cell = lax.axis_index("cell").astype(jnp.int32)
    my_view = lax.axis_index("view").astype(jnp.int32)
    me = jnp.stack([my_cell * groups + my_view, my_cell, my_view])
    down_pairs = [(s, (s + 1) % cells) for s in range(cells) if (s - quarter) % half != half - 1]
    up_pairs = [(b, a) for a, b in down_pairs]
    target_up = lax.ppermute(target[0, :, 11:16, :], "cell", down_pairs)
    target_down = lax.ppermute(target[0, :, 0:5, :], "cell", up_pairs)

    lists = jnp.swapaxes(tile_blocks[0, 0], 0, 1)
    table = jnp.concatenate([lists, tile_ids[0]], axis=0)
    table = lax.all_to_all(
        jnp.broadcast_to(table, (devices, length + 1, tiles)),
        ("cell", "view"), split_axis=0, concat_axis=0, tiled=True,
    )
    work = blocks * GBLK * 10000
    feats, route = call(
        functools.partial(prepare_kernel, cells, groups, cap, rcap, per_row),
        (shape((visible.shape[0], 9, rows, GBLK), F32), shape((8, LANES), jnp.int32)),
        [SMEM] + [VMEM] * 4,
        [VMEM((LANES, LANES), F32), VMEM((512, LANES), F32), VMEM((64, LANES), jnp.int32)],
        32, work,
    )(cameras, tile_ids[0], lists, gauss_params, visible)
    made, code = call(
        functools.partial(render_kernel, cells, groups, cap, rcap, per_row, blocks),
        (shape((devices, 8 * cap, LANES), F32), shape((devices, LANES), jnp.int32)),
        [SMEM, VMEM, VMEM, pl.ANY, pl.ANY],
        [
            VMEM((length + 1, devices, LANES), F32),
            VMEM((2 * LANES, LANES), F32),
            VMEM((2, 9, LANES, LANES), F32),
            VMEM((1024, LANES), F32),
            VMEM((256, LANES), F32),
            VMEM((rows * 8, LANES), F32),
            VMEM((devices, LANES), jnp.int32),
            SMEM((devices, LANES), jnp.int32),
            pltpu.SemaphoreType.DMA,
        ],
        32, work,
    )(me, table, feats, target_up, target_down)
    got = lax.all_to_all(made, ("cell", "view"), split_axis=0, concat_axis=0, tiled=True)
    planes = shape((1, 3, 16, width), F32)
    fixed = call(
        target_kernel,
        shape((2, 3, 16, width), F32),
        [VMEM] * 3 + [pl.ANY],
        [VMEM((2, 32, LANES), F32), VMEM((2, 16, width + 2 * LANES), F32)],
        16, work,
    )(target, target_up, target_down, made)
    tile_rows = call(
        functools.partial(combine_kernel, tiles),
        shape((cells * 6 * rcap, LANES), F32),
        [SMEM, VMEM, pl.ANY],
    )(route, got.reshape(devices * cap * 8, LANES), fixed)
    got_tiles = lax.all_to_all(
        tile_rows.reshape(cells, 6 * rcap, LANES), "cell", split_axis=0, concat_axis=0, tiled=True
    )
    edge = shape((3, 5, width), F32)
    image, head, tail = call(
        functools.partial(place_kernel, groups, cap, rcap, per_row),
        (planes, edge, edge),
        [SMEM, SMEM, VMEM],
        [VMEM((8 * (per_row + 1), LANES), F32)],
    )(code, me, got_tiles)
    up_rows = lax.ppermute(tail, "cell", down_pairs)
    down_rows = lax.ppermute(head, "cell", up_pairs)
    blur_room = [VMEM((3, 32, LANES), F32), VMEM((3, 16, width + 2 * LANES), F32)]
    own = call(
        own_kernel, shape((3, 3, 16, width), F32), [VMEM] * 2, blur_room, 16, work
    )(image, target)
    return call(
        loss_kernel, (planes, shape((1, 16, width), F32)), [VMEM] * 8, blur_room, 24
    )(image, target, own, fixed, up_rows, down_rows, target_up, target_down)


def solution(mesh):
    return jax.shard_map(
        local,
        mesh=mesh,
        in_specs=(
            P(None, ("cell", "view")),
            P(None, ("cell", "view")),
            P(),
            P("cell", "view", None),
            P("cell", "view", None, None),
            P("view", None, "cell", None),
        ),
        out_specs=(P("view", None, "cell", None), P("view", "cell", None)),
        check_vma=False,
    )
```

time: 338 us -> 113 us (0.33); the launches traced: 333 us -> 112 us
  matrix products: 95.4 us -> 0 us
  other arithmetic: 83.1 us -> 0.78 us
  local copies, waits for them, and re-layouts: 78.9 us -> 10.5 us
  Pallas kernels: 0 us -> 36.7 us
  waiting for transfers between devices: 35.9 us -> 14.4 us
  blocking collectives: 8.51 us -> 17.1 us
    dot_general x4 -> x0, matrix products: 95.4 us -> none  [the longest x2 55.3 us: blend_slot(): jnp.einsum('tpg,tcg->tcp', weights, features[:, 6:9], precision=lax.Preci...]
    add x9 -> x0, other arithmetic: 45.1 us -> none  [the longest x1 19.4 us: blur(): sum((taps[number] * across[..., number:number + row_count, :] for number...]
    pallas_call x0 -> x7, Pallas kernels: none -> 36.7 us  [the longest x1 14.6 us: local(): call(functools.partial(render_kernel, cells, groups, cap, rcap, per_row,...]
    slice x10 -> x0, local copies, waits for them, and re-layouts: 25 us -> none  [the longest x3 20.8 us: project(): raw_params[:, 11 + 3 * number + channel]]
    reduce_sum x7 -> x0, other arithmetic: 20.3 us -> none  [the longest x1 17 us: blend_slot(): return (log_trans + jnp.sum(log_keep, axis=2), colour)]
    ppermute x2 -> x4, starting transfers between devices: 2.26 us -> 18.7 us  [the longest x1 7.38 us: local(): target_down = lax.ppermute(target[0, :, 0:5, :], 'cell', up_pairs)]
    all_to_all x4 -> x2, starting transfers between devices: 27.1 us -> 13.3 us  [the longest x1 7.3 us: local(): lax.all_to_all(jnp.broadcast_to(table, (devices, length + 1, tiles)), ('c...]
    reshape x7 -> x0, local copies, waits for them, and re-layouts: 12.9 us -> none  [the longest x2 10.7 us: request_lookup(): gauss_params.reshape(gauss_params.shape[0], blocks, GBLK)[:, local_slot]]
  transfers between devices with their start and end apart: 6 -> 6, of which waited for: 4 -> 1; matrix products, arithmetic and copies ran while one was open for 43% -> 1% of each run, Pallas kernels for 0% -> 12%
where the time goes in v1:
time: 113 us; the launch traced here: 112 us
  Pallas kernels  36.7 us (32%)
  starting transfers between devices  32 us (28%)
  blocking collectives  17.1 us (15%)
  waiting for transfers between devices  14.4 us (13%)
  local copies, waits for them, and re-layouts  10.5 us (9%)
    all_to_all x1, blocking collectives, local(): lax.all_to_all(tile_rows.reshape(cells, 6 * rcap, LANES), 'cell', split_a...  17.1 us
    pallas_call x1, Pallas kernels, local(): call(functools.partial(render_kernel, cells, groups, cap, rcap, per_row,...  14.6 us
    all_to_all x1, waiting for transfers between devices, local(): lax.all_to_all(made, ('cell', 'view'), split_axis=0, concat_axis=0, tiled...  14.4 us
    unnamed x16, local copies, waits for them, and re-layouts  8.81 us
    ppermute x1, starting transfers between devices, local(): target_down = lax.ppermute(target[0, :, 0:5, :], 'cell', up_pairs)  7.38 us
    all_to_all x1, starting transfers between devices, local(): lax.all_to_all(jnp.broadcast_to(table, (devices, length + 1, tiles)), ('c...  7.3 us
    ppermute x1, starting transfers between devices, local(): down_rows = lax.ppermute(head, 'cell', up_pairs)  6.97 us
    all_to_all x1, starting transfers between devices, local(): lax.all_to_all(made, ('cell', 'view'), split_axis=0, concat_axis=0, tiled...  5.98 us
  transfers between devices with their start and end apart: 6, of which 1 were waited for; matrix products, arithmetic and copies ran while one was open for 1% of the time, Pallas kernels for 12%

profile of v1, /device:TPU:0, one launch (start us, length us, event | category | flops | bytes accessed | tf_op | source)
XLA Modules:
  0.0 112.2 jit_solution(8514477262875511938)
XLA Ops:
  0.6 0.7 pad_add_fusion
  1.3 0.6 broadcast_in_dim.3
  2.0 7.3 %all-to-all-start = ((s32[32,3,120]{2,1,0:T(4,128)}), s32[32,3,120]{2,1,0:T(4,128)S(1)}, u32[]{:S(2)}, u32[]{:S(2)}) async-start(s32[32,3,120]{2,1,0:T(4,128)} %broadcast_in_dim.3), calls=%async_computation | async-start | bytes 131072 | tf_op jit(solution)/shard_map/all_to_all | solution.py:540
  9.3 1.0 slice_bitcast_fusion
  10.3 7.4 %collective-permute-start.1 = (f32[3,5,1920]{2,1,0:T(8,128)S(1)}, f32[3,5,1920]{2,1,0:T(8,128)S(1)}, u32[]{:S(2)}, u32[]{:S(2)}) collective-permute-start(f32[3,5,1920]{2,1,0:T(8,128)S(1)} %get-tuple-element.16), channel_id=1, source_target_pairs={{2,0},{4,2},{6,4},{10,8},{12,10},{14,12},{16,14},{18,16},{20,18},{... | collective-permute-start | bytes 345608 | tf_op jit(solution)/shard_map/ppermute | solution.py:536
  17.7 1.9 %collective-permute-start = (f32[3,5,1920]{2,1,0:T(8,128)S(1)}, f32[3,5,1920]{2,1,0:T(8,128)S(1)}, u32[]{:S(2)}, u32[]{:S(2)}) collective-permute-start(f32[3,5,1920]{2,1,0:T(8,128)S(1)} %get-tuple-element.17), channel_id=1, source_target_pairs={{0,2},{2,4},{4,6},{8,10},{10,12},{12,14},{14,16},{16,18},{18,20},{... | collective-permute-start | bytes 345608 | tf_op jit(solution)/shard_map/ppermute | solution.py:535
  19.6 0.0 copy-start.1
  19.6 2.4 %copy-done.1 = f32[59,19200]{1,0:T(8,128)S(1)} copy-done((f32[59,19200]{1,0:T(8,128)S(1)}, f32[59,19200]{1,0:T(8,128)}, u32[]{:S(2)}) %copy-start.1) | copy-done | bytes 4531224
  22.0 1.0 copy-done.4
  23.0 0.7 copy-done.5
  23.7 0.7 copy-done.6
  24.4 0.7 copy-done.7
  25.0 5.5 %shard_map.77 = (f32[4,9,160,128]{3,2,1,0:T(8,128)S(1)}, s32[8,128]{1,0:T(8,128)S(1)}) custom-call(f32[4,15]{1,0:T(4,128)S(1)} %copy-done.6, s32[1,120]{1,0:T(1,128)S(1)} %bitcast.18, s32[2,120]{1,0:T(2,128)S(1)} %bitcast.16, f32[59,19200]{1,0:T(8,128)S(1)} %copy-done.1, s32[4,19200]{1,0:T(4,128)S(1)} %copy-done.4), custom_call_target="tpu_custom_call" | custom-call | flops 192000000 | tf_op jit(solution)/shard_map/pallas_call | solution.py:545
  30.5 1.6 %copy-done.2 = f32[4,9,160,128]{3,2,1,0:T(8,128)} copy-done((f32[4,9,160,128]{3,2,1,0:T(8,128)}, f32[4,9,160,128]{3,2,1,0:T(8,128)S(1)}, u32[]{:S(2)}) %copy-start.2) | copy-done | bytes 2949144
  32.1 0.1 pad_add_fusion.1.me_ref
  32.2 0.0 all-to-all-done.table_ref
  32.2 0.0 collective-permute-done.1.early_down.down_ref.target_down
  32.2 0.0 collective-permute-done.early_up.up_ref.target_up
  32.2 1.9 %copy-done.3 = f32[4,9,160,128]{3,2,1,0:T(8,128)S(1)} copy-done((f32[4,9,160,128]{3,2,1,0:T(8,128)S(1)}, f32[4,9,160,128]{3,2,1,0:T(8,128)}, u32[]{:S(2)}) %copy-start.3) | copy-done | bytes 2949144
  34.1 14.6 %shard_map.78 = (f32[32,40,128]{2,1,0:T(8,128)}, s32[32,128]{1,0:T(8,128)S(1)}) custom-call(s32[3]{0:T(128)S(1)} %pad_add_fusion.1.me_ref, s32[32,3,120]{2,1,0:T(4,128)S(1)} %all-to-all-done.table_ref, f32[4,9,160,128]{3,2,1,0:T(8,128)S(1)} %copy-done.3, f32[3,5,1920]{2,1,0:T(8,128)S(1)} %collective-permute-done.early_up.up_ref.target_up, ...), custom_call_target="tpu_custom_call" | custom-call | flops 192000000 | tf_op jit(solution)/shard_map/pallas_call | solution.py:552
  48.7 6.0 %all-to-all-start.1 = ((f32[32,40,128]{2,1,0:T(8,128)}), f32[32,40,128]{2,1,0:T(8,128)S(1)}, u32[]{:S(2)}, u32[]{:S(2)}) async-start(f32[32,40,128]{2,1,0:T(8,128)} %get-tuple-element.12.late_ref), calls=%async_computation.1 | async-start | bytes 1310720 | tf_op jit(solution)/shard_map/all_to_all | solution.py:569
  54.7 3.5 %shard_map.79.fixed_ref = f32[2,3,16,1920]{3,2,1,0:T(8,128)S(1)} custom-call(f32[1,3,16,1920]{3,2,1,0:T(8,128)S(1)} %copy-done, f32[3,5,1920]{2,1,0:T(8,128)S(1)} %collective-permute-done.early_up.up_ref.target_up, f32[3,5,1920]{2,1,0:T(8,128)S(1)} %collective-permute-done.1.early_down.down_ref.target_down, f32[32,40,128]{2,1,0:T(8,128)} %get-tuple-element.12.late_ref), custom_call_target="tpu_custom_call" | custom-call | flops 192000000 | tf_op jit(solution)/shard_map/pallas_call | solution.py:571
  58.2 14.4 %all-to-all-done.1 = f32[32,40,128]{2,1,0:T(8,128)S(1)} async-done(((f32[32,40,128]{2,1,0:T(8,128)}), f32[32,40,128]{2,1,0:T(8,128)S(1)}, u32[]{:S(2)}, u32[]{:S(2)}) %all-to-all-start.1) | async-done | bytes 655392 | tf_op jit(solution)/shard_map/all_to_all | solution.py:569
  72.6 1.4 %shard_map.80 = f32[768,128]{1,0:T(8,128)S(1)} custom-call(s32[8,128]{1,0:T(8,128)S(1)} %get-tuple-element.11.route_ref, f32[1280,128]{1,0:T(8,128)S(1)} %bitcast.13, f32[2,3,16,1920]{3,2,1,0:T(8,128)S(1)} %shard_map.79.fixed_ref), custom_call_target="tpu_custom_call" | custom-call | tf_op jit(solution)/shard_map/pallas_call | solution.py:578
  74.0 17.1 %all_to_all.15.got_ref = f32[16,48,128]{2,1,0:T(8,128)S(1)} all-to-all(f32[16,48,128]{2,1,0:T(8,128)S(1)} %bitcast.14), channel_id=1, replica_groups=mesh['cell'=16,'view'=2] {'cell'}, dimensions={0} | all-to-all | bytes 786432 | tf_op jit(solution)/shard_map/all_to_all | solution.py:583
  91.1 1.6 %shard_map.81 = (f32[1,3,16,1920]{3,2,1,0:T(8,128)S(1)}, f32[3,5,1920]{2,1,0:T(8,128)S(1)}, f32[3,5,1920]{2,1,0:T(8,128)S(1)}) custom-call(s32[32,128]{1,0:T(8,128)S(1)} %get-tuple-element.10.code_ref, s32[3]{0:T(128)S(1)} %pad_add_fusion.1.me_ref, f32[16,48,128]{2,1,0:T(8,128)S(1)} %all_to_all.15.got_ref), custom_call_target="tpu_custom_call" | custom-call | tf_op jit(solution)/shard_map/pallas_call | solution.py:587
  92.6 2.5 %collective-permute-start.2 = (f32[3,5,1920]{2,1,0:T(8,128)S(1)}, f32[3,5,1920]{2,1,0:T(8,128)S(1)}, u32[]{:S(2)}, u32[]{:S(2)}) collective-permute-start(f32[3,5,1920]{2,1,0:T(8,128)S(1)} %get-tuple-element.14), channel_id=1, source_target_pairs={{0,2},{2,4},{4,6},{8,10},{10,12},{12,14},{14,16},{16,18},{18,20},{... | collective-permute-start | bytes 345608 | tf_op jit(solution)/shard_map/ppermute | solution.py:593
  95.1 7.0 %collective-permute-start.3 = (f32[3,5,1920]{2,1,0:T(8,128)S(1)}, f32[3,5,1920]{2,1,0:T(8,128)S(1)}, u32[]{:S(2)}, u32[]{:S(2)}) collective-permute-start(f32[3,5,1920]{2,1,0:T(8,128)S(1)} %get-tuple-element.15), channel_id=1, source_target_pairs={{2,0},{4,2},{6,4},{10,8},{12,10},{14,12},{16,14},{18,16},{20,18},{... | collective-permute-start | bytes 345608 | tf_op jit(solution)/shard_map/ppermute | solution.py:594
  102.1 4.7 %shard_map.82.own_ref = f32[3,3,16,1920]{3,2,1,0:T(8,128)S(1)} custom-call(f32[1,3,16,1920]{3,2,1,0:T(8,128)S(1)} %get-tuple-element.13.image_ref, f32[1,3,16,1920]{3,2,1,0:T(8,128)S(1)} %copy-done), custom_call_target="tpu_custom_call" | custom-call | flops 192000000 | tf_op jit(solution)/shard_map/pallas_call | solution.py:596
  106.8 0.0 collective-permute-done.2.up_ref
  106.8 0.0 collective-permute-done.3.down_ref
  106.9 5.4 %shard_map.83 = (f32[1,3,16,1920]{3,2,1,0:T(8,128)}, f32[1,16,1920]{2,1,0:T(8,128)}) custom-call(f32[1,3,16,1920]{3,2,1,0:T(8,128)S(1)} %get-tuple-element.13.image_ref, f32[1,3,16,1920]{3,2,1,0:T(8,128)S(1)} %copy-done, f32[3,3,16,1920]{3,2,1,0:T(8,128)S(1)} %shard_map.82.own_ref, f32[2,3,16,1920]{3,2,1,0:T(8,128)S(1)} %shard_map.79.fixed_ref, ...), custom_call_target="tpu_custom_call" | custom-call | tf_op jit(solution)/shard_map/pallas_call | solution.py:599
  (8 shorter events, 0.0 us)
Async XLA Ops:
  2.0 30.2 %all-to-all-start = ((s32[32,3,120]{2,1,0:T(4,128)}), s32[32,3,120]{2,1,0:T(4,128)S(1)}, u32[]{:S(2)}, u32[]{:S(2)}) async-start(s32[32,3,120]{2,1,0:T(4,128)} %broadcast_in_dim.3), calls=%async_computation | async-start | bytes 131072 | tf_op jit(solution)/shard_map/all_to_all | solution.py:540
  10.3 21.9 %collective-permute-start.1 = (f32[3,5,1920]{2,1,0:T(8,128)S(1)}, f32[3,5,1920]{2,1,0:T(8,128)S(1)}, u32[]{:S(2)}, u32[]{:S(2)}) collective-permute-start(f32[3,5,1920]{2,1,0:T(8,128)S(1)} %get-tuple-element.16), channel_id=1, source_target_pairs={{2,0},{4,2},{6,4},{10,8},{12,10},{14,12},{16,14},{18,16},{20,18},{... | collective-permute-start | bytes 345608 | tf_op jit(solution)/shard_map/ppermute | solution.py:536
  17.7 14.5 %collective-permute-start = (f32[3,5,1920]{2,1,0:T(8,128)S(1)}, f32[3,5,1920]{2,1,0:T(8,128)S(1)}, u32[]{:S(2)}, u32[]{:S(2)}) collective-permute-start(f32[3,5,1920]{2,1,0:T(8,128)S(1)} %get-tuple-element.17), channel_id=1, source_target_pairs={{0,2},{2,4},{4,6},{8,10},{10,12},{12,14},{14,16},{16,18},{18,20},{... | collective-permute-start | bytes 345608 | tf_op jit(solution)/shard_map/ppermute | solution.py:535
  19.6 2.4 %copy-start.1 = (f32[59,19200]{1,0:T(8,128)S(1)}, f32[59,19200]{1,0:T(8,128)}, u32[]{:S(2)}) copy-start(f32[59,19200]{1,0:T(8,128)} %params_ref.1) | copy-start | bytes 13593604
  22.0 1.0 copy-start.4
  23.0 0.7 copy-start.5
  23.7 0.7 copy-start.6
  24.4 0.7 copy-start.7
  30.5 1.6 %copy-start.2 = (f32[4,9,160,128]{3,2,1,0:T(8,128)}, f32[4,9,160,128]{3,2,1,0:T(8,128)S(1)}, u32[]{:S(2)}) copy-start(f32[4,9,160,128]{3,2,1,0:T(8,128)S(1)} %get-tuple-element.9.feats_ref) | copy-start | bytes 8847364
  32.1 22.6 %copy-start = (f32[1,3,16,1920]{3,2,1,0:T(8,128)S(1)}, f32[1,3,16,1920]{3,2,1,0:T(8,128)}, u32[]{:S(2)}) copy-start(f32[1,3,16,1920]{3,2,1,0:T(8,128)} %target_ref.5) | copy-start | bytes 1105924
  32.2 1.9 %copy-start.3 = (f32[4,9,160,128]{3,2,1,0:T(8,128)S(1)}, f32[4,9,160,128]{3,2,1,0:T(8,128)}, u32[]{:S(2)}) copy-start(f32[4,9,160,128]{3,2,1,0:T(8,128)} %copy-done.2) | copy-start | bytes 8847364
  48.7 23.9 %all-to-all-start.1 = ((f32[32,40,128]{2,1,0:T(8,128)}), f32[32,40,128]{2,1,0:T(8,128)S(1)}, u32[]{:S(2)}, u32[]{:S(2)}) async-start(f32[32,40,128]{2,1,0:T(8,128)} %get-tuple-element.12.late_ref), calls=%async_computation.1 | async-start | bytes 1310720 | tf_op jit(solution)/shard_map/all_to_all | solution.py:569
  92.6 14.2 %collective-permute-start.2 = (f32[3,5,1920]{2,1,0:T(8,128)S(1)}, f32[3,5,1920]{2,1,0:T(8,128)S(1)}, u32[]{:S(2)}, u32[]{:S(2)}) collective-permute-start(f32[3,5,1920]{2,1,0:T(8,128)S(1)} %get-tuple-element.14), channel_id=1, source_target_pairs={{0,2},{2,4},{4,6},{8,10},{10,12},{12,14},{14,16},{16,18},{18,20},{... | collective-permute-start | bytes 345608 | tf_op jit(solution)/shard_map/ppermute | solution.py:593
  95.1 11.7 %collective-permute-start.3 = (f32[3,5,1920]{2,1,0:T(8,128)S(1)}, f32[3,5,1920]{2,1,0:T(8,128)S(1)}, u32[]{:S(2)}, u32[]{:S(2)}) collective-permute-start(f32[3,5,1920]{2,1,0:T(8,128)S(1)} %get-tuple-element.15), channel_id=1, source_target_pairs={{2,0},{4,2},{6,4},{10,8},{12,10},{14,12},{16,14},{18,16},{20,18},{... | collective-permute-start | bytes 345608 | tf_op jit(solution)/shard_map/ppermute | solution.py:594

commit v2 on v1

--- a/solution.py
+++ b/solution.py
@@ -13,6 +13,8 @@
 LOG2E = math.log2(math.e)
 VMEM = pltpu.VMEM
 SMEM = pltpu.SMEM
+HBM = pltpu.HBM
+PIECES = 4
 F32 = jnp.float32
 
 
@@ -25,11 +27,10 @@
     return whole, value - whole * size
 
 
-def own_route(cells, groups, blocks, cap, rcap, per_row, ids_ref, lists_ref, route_ref, box):
-    length, tiles = lists_ref.shape
+def own_route(cells, groups, blocks, cap, rcap, per_row, table_ref, route_ref, box):
+    length, tiles = table_ref.shape[0] - 1, table_ref.shape[1]
     box[...] = jnp.full(box.shape, -1.0, F32)
-    box[0:length, 0:tiles] = lists_ref[...].astype(F32)
-    box[length : length + 1, 0:tiles] = ids_ref[...].astype(F32)
+    box[0 : length + 1, 0:tiles] = table_ref[...].astype(F32)
     rows = box[...]
     columns = rows.T
     earlier = iota((LANES, LANES), 1) < iota((LANES, LANES), 0)
@@ -143,15 +144,28 @@
 
 def prepare_kernel(
     cells, groups, cap, rcap, per_row,
-    cams_ref, ids_ref, lists_ref, params_ref, seen_ref, feats_ref, route_ref, box, stage, seen_stage,
+    cams_ref, table_ref, params_hbm, seen_hbm, feats_ref, route_ref,
+    box, stage, seen_stage, params_ref, seen_ref, sems,
 ):
     features, total = params_ref.shape
     blocks = total // GBLK
     views = seen_ref.shape[0]
-    own_route(cells, groups, blocks, cap, rcap, per_row, ids_ref, lists_ref, route_ref, box)
-
-    @pl.loop(0, -(-blocks // 8))
-    def _(group):
+    seen_copy = pltpu.make_async_copy(seen_hbm, seen_ref, sems.at[PIECES])
+    seen_copy.start()
+    groups_all = -(-blocks // 8)
+    per_piece = -(-groups_all // PIECES)
+    copies = []
+    for piece in range(PIECES):
+        low = piece * per_piece * 8 * GBLK
+        lanes = pl.ds(low, min(per_piece * 8 * GBLK, total - low))
+        copies.append(
+            pltpu.make_async_copy(params_hbm.at[:, lanes], params_ref.at[:, lanes], sems.at[piece])
+        )
+        copies[-1].start()
+    own_route(cells, groups, blocks, cap, rcap, per_row, table_ref, route_ref, box)
+    seen_copy.wait()
+
+    def project_group(group):
         first = jnp.minimum(8 * group, blocks - 8)
         for b in range(8):
             lanes = pl.ds(pl.multiple_of((first + b) * GBLK, GBLK), GBLK)
@@ -170,13 +184,18 @@
             for number, value in enumerate(made):
                 feats_ref[view, number, pl.ds(first, 8), :] = value
 
+    for piece in range(PIECES):
+        copies[piece].wait()
+        pl.loop(piece * per_piece, min((piece + 1) * per_piece, groups_all))(project_group)
+
 
 def render_kernel(
     cells, groups, cap, rcap, per_row, blocks,
-    me_ref, table_ref, feats_ref, early_up, early_down, out_ref, code_ref,
+    me_ref, table_ref, feats_ref, target_ref, out_ref, code_ref, head_ref, tail_ref,
     box, info, turned, shades, rest, sheets, code_box, code_smem, sem,
 ):
-    del early_up, early_down
+    head_ref[...] = target_ref[0, :, 0:5, :]
+    tail_ref[...] = target_ref[0, :, 11:16, :]
     devices = cells * groups
     quarter, half = cells // 4, cells // 2
     length, tiles = table_ref.shape[1] - 1, table_ref.shape[2]
@@ -379,9 +398,16 @@
     blurred = []
     for f in range(tall.shape[0]):
         given = tall[f, :, LANES * first : LANES * first + around]
-        total = taps[0] * given
-        for k in range(1, 6):
-            total = total + taps[k] * (pltpu.roll(given, k, 1) + pltpu.roll(given, around - k, 1))
+        near = [pltpu.roll(given, 1, 1), given, pltpu.roll(given, around - 1, 1), pltpu.roll(given, around - 2, 1)]
+        far = []
+        for a in range(3):
+            total = None
+            for b in range(4):
+                if 4 * a + b < 11:
+                    term = taps[abs(4 * a + b - 5)] * near[b]
+                    total = term if total is None else total + term
+            far.append(total)
+        total = pltpu.roll(far[0], 4, 1) + far[1] + pltpu.roll(far[2], around - 4, 1)
         blurred.append(total[:, LANES : LANES + count * LANES])
     return blurred
 
@@ -407,8 +433,7 @@
 RUN = 5
 
 
-def target_kernel(target_ref, up_ref, down_ref, late_ref, out_ref, fields, tall):
-    del late_ref
+def target_kernel(target_ref, up_ref, down_ref, out_ref, fields, tall):
     spans = target_ref.shape[3] // LANES
     clear_sides(tall)
 
@@ -501,7 +526,7 @@
             loss_ref[0, :, lanes] = jnp.where(c == 0, 0.2, loss_ref[0, :, lanes]) + part
 
 
-def call(kernel, outs, specs, scratch=(), mem=16, work=0):
+def call(kernel, outs, specs, scratch=(), mem=8, work=0):
     return pl.pallas_call(
         kernel,
         out_shape=outs,
@@ -532,27 +557,32 @@
     me = jnp.stack([my_cell * groups + my_view, my_cell, my_view])
     down_pairs = [(s, (s + 1) % cells) for s in range(cells) if (s - quarter) % half != half - 1]
     up_pairs = [(b, a) for a, b in down_pairs]
-    target_up = lax.ppermute(target[0, :, 11:16, :], "cell", down_pairs)
-    target_down = lax.ppermute(target[0, :, 0:5, :], "cell", up_pairs)
-
     lists = jnp.swapaxes(tile_blocks[0, 0], 0, 1)
-    table = jnp.concatenate([lists, tile_ids[0]], axis=0)
+    own_table = jnp.concatenate([lists, tile_ids[0]], axis=0)
     table = lax.all_to_all(
-        jnp.broadcast_to(table, (devices, length + 1, tiles)),
+        jnp.broadcast_to(own_table, (devices, length + 1, tiles)),
         ("cell", "view"), split_axis=0, concat_axis=0, tiled=True,
     )
     work = blocks * GBLK * 10000
     feats, route = call(
         functools.partial(prepare_kernel, cells, groups, cap, rcap, per_row),
         (shape((visible.shape[0], 9, rows, GBLK), F32), shape((8, LANES), jnp.int32)),
-        [SMEM] + [VMEM] * 4,
-        [VMEM((LANES, LANES), F32), VMEM((512, LANES), F32), VMEM((64, LANES), jnp.int32)],
-        32, work,
-    )(cameras, tile_ids[0], lists, gauss_params, visible)
-    made, code = call(
+        [SMEM, VMEM, HBM, HBM],
+        [
+            VMEM((LANES, LANES), F32),
+            VMEM((512, LANES), F32),
+            VMEM((64, LANES), jnp.int32),
+            VMEM(gauss_params.shape, F32),
+            VMEM(visible.shape, jnp.int32),
+            pltpu.SemaphoreType.DMA((PIECES + 1,)),
+        ],
+        50, work,
+    )(cameras, own_table, gauss_params, visible)
+    edge = shape((3, 5, width), F32)
+    made, code, target_head, target_tail = call(
         functools.partial(render_kernel, cells, groups, cap, rcap, per_row, blocks),
-        (shape((devices, 8 * cap, LANES), F32), shape((devices, LANES), jnp.int32)),
-        [SMEM, VMEM, VMEM, pl.ANY, pl.ANY],
+        (shape((devices, 8 * cap, LANES), F32), shape((devices, LANES), jnp.int32), edge, edge),
+        [SMEM, VMEM, VMEM, VMEM],
         [
             VMEM((length + 1, devices, LANES), F32),
             VMEM((2 * LANES, LANES), F32),
@@ -564,17 +594,19 @@
             SMEM((devices, LANES), jnp.int32),
             pltpu.SemaphoreType.DMA,
         ],
-        32, work,
-    )(me, table, feats, target_up, target_down)
+        12, work,
+    )(me, table, feats, target)
+    target_up = lax.ppermute(target_tail, "cell", down_pairs)
+    target_down = lax.ppermute(target_head, "cell", up_pairs)
     got = lax.all_to_all(made, ("cell", "view"), split_axis=0, concat_axis=0, tiled=True)
     planes = shape((1, 3, 16, width), F32)
     fixed = call(
         target_kernel,
         shape((2, 3, 16, width), F32),
-        [VMEM] * 3 + [pl.ANY],
+        [VMEM] * 3,
         [VMEM((2, 32, LANES), F32), VMEM((2, 16, width + 2 * LANES), F32)],
-        16, work,
-    )(target, target_up, target_down, made)
+        8, work,
+    )(target, target_up, target_down)
     tile_rows = call(
         functools.partial(combine_kernel, tiles),
         shape((cells * 6 * rcap, LANES), F32),
@@ -583,7 +615,6 @@
     got_tiles = lax.all_to_all(
         tile_rows.reshape(cells, 6 * rcap, LANES), "cell", split_axis=0, concat_axis=0, tiled=True
     )
-    edge = shape((3, 5, width), F32)
     image, head, tail = call(
         functools.partial(place_kernel, groups, cap, rcap, per_row),
         (planes, edge, edge),
@@ -594,10 +625,10 @@
     down_rows = lax.ppermute(head, "cell", up_pairs)
     blur_room = [VMEM((3, 32, LANES), F32), VMEM((3, 16, width + 2 * LANES), F32)]
     own = call(
-        own_kernel, shape((3, 3, 16, width), F32), [VMEM] * 2, blur_room, 16, work
+        own_kernel, shape((3, 3, 16, width), F32), [VMEM] * 2, blur_room, 8, work
     )(image, target)
     return call(
-        loss_kernel, (planes, shape((1, 16, width), F32)), [VMEM] * 8, blur_room, 24
+        loss_kernel, (planes, shape((1, 16, width), F32)), [VMEM] * 8, blur_room, 8
     )(image, target, own, fixed, up_rows, down_rows, target_up, target_down)
 
 

time: 113 us -> 106 us (0.938)
  local copies, waits for them, and re-layouts: 10.5 us -> 5.7 us
  waiting for transfers between devices: 14.4 us -> 11.8 us
    all_to_all x1, waiting for transfers between devices: 14.4 us -> 0.01 us  [local(): lax.all_to_all(made, ('cell', 'view'), split_axis=0, concat_axis=0, tiled...]
    ppermute x2, waiting for transfers between devices: 0.01 us -> 11.8 us  [the longest x1 11.7 us: local(): target_up = lax.ppermute(target_tail, 'cell', down_pairs)]
    unnamed x16 -> x10, local copies, waits for them, and re-layouts: 8.81 us -> 5.06 us
  transfers between devices with their start and end apart: 6 -> 6, of which waited for: 1 -> 1; matrix products, arithmetic and copies ran while one was open for 1% -> 0% of each run, Pallas kernels for 12% -> 14%
where the time goes in v2:
time: 106 us; the launch traced here: 105 us
  Pallas kernels  37.3 us (35%)
  starting transfers between devices  32 us (30%)
  blocking collectives  16.9 us (16%)
  waiting for transfers between devices  11.8 us (11%)
  local copies, waits for them, and re-layouts  5.7 us (5%)
    all_to_all x1, blocking collectives, local(): lax.all_to_all(tile_rows.reshape(cells, 6 * rcap, LANES), 'cell', split_a...  16.9 us
    pallas_call x1, Pallas kernels, local(): call(functools.partial(render_kernel, cells, groups, cap, rcap, per_row,...  14.6 us
    ppermute x1, waiting for transfers between devices, local(): target_up = lax.ppermute(target_tail, 'cell', down_pairs)  11.7 us
    all_to_all x1, starting transfers between devices, local(): lax.all_to_all(jnp.broadcast_to(own_table, (devices, length + 1, tiles)),...  7.3 us
    ppermute x1, starting transfers between devices, local(): down_rows = lax.ppermute(head, 'cell', up_pairs)  6.97 us
    pallas_call x1, Pallas kernels, local(): call(functools.partial(prepare_kernel, cells, groups, cap, rcap, per_row)...  6.37 us
    all_to_all x1, starting transfers between devices, local(): lax.all_to_all(made, ('cell', 'view'), split_axis=0, concat_axis=0, tiled...  5.84 us
    ppermute x1, starting transfers between devices, local(): target_down = lax.ppermute(target_head, 'cell', up_pairs)  5.76 us
  transfers between devices with their start and end apart: 6, of which 1 were waited for; matrix products, arithmetic and copies ran while one was open for 0% of the time, Pallas kernels for 14%

profile of v2, /device:TPU:0, one launch (start us, length us, event | category | flops | bytes accessed | tf_op | source)
XLA Modules:
  0.0 105.3 jit_solution(2032498529964377105)
XLA Ops:
  0.6 0.0 copy-start
  0.6 0.8 pad_add_fusion.table_ref
  1.4 0.6 broadcast_in_dim.3
  2.0 7.3 %all-to-all-start = ((s32[32,3,120]{2,1,0:T(4,128)}), s32[32,3,120]{2,1,0:T(4,128)S(1)}, u32[]{:S(2)}, u32[]{:S(2)}) async-start(s32[32,3,120]{2,1,0:T(4,128)} %broadcast_in_dim.3), calls=%async_computation | async-start | bytes 131072 | tf_op jit(solution)/shard_map/all_to_all | solution.py:562
  9.3 0.0 copy-start.3
  9.4 1.0 copy-done.3
  10.3 0.0 copy-start.4
  10.3 0.7 copy-done.4
  11.0 6.4 %shard_map.77 = (f32[4,9,160,128]{3,2,1,0:T(8,128)S(1)}, s32[8,128]{1,0:T(8,128)S(1)}) custom-call(f32[4,15]{1,0:T(4,128)S(1)} %copy-done.4, s32[3,120]{1,0:T(4,128)S(1)} %pad_add_fusion.table_ref, f32[59,19200]{1,0:T(8,128)} %params_hbm.1, s32[4,19200]{1,0:T(4,128)S(1)} %copy-done.3), custom_call_target="tpu_custom_call" | custom-call | flops 192000000 | tf_op jit(solution)/shard_map/pallas_call | solution.py:567
  17.4 0.0 copy-start.1
  17.4 1.6 %copy-done.1 = f32[4,9,160,128]{3,2,1,0:T(8,128)} copy-done((f32[4,9,160,128]{3,2,1,0:T(8,128)}, f32[4,9,160,128]{3,2,1,0:T(8,128)S(1)}, u32[]{:S(2)}) %copy-start.1) | copy-done | bytes 2949144
  19.0 0.1 pad_add_fusion.1.me_ref
  19.0 0.0 all-to-all-done.table_ref
  19.0 0.0 copy-done
  19.0 1.8 %copy-done.2 = f32[4,9,160,128]{3,2,1,0:T(8,128)S(1)} copy-done((f32[4,9,160,128]{3,2,1,0:T(8,128)S(1)}, f32[4,9,160,128]{3,2,1,0:T(8,128)}, u32[]{:S(2)}) %copy-start.2) | copy-done | bytes 2949144
  20.9 14.6 %shard_map.78 = (f32[32,40,128]{2,1,0:T(8,128)}, s32[32,128]{1,0:T(8,128)S(1)}, f32[3,5,1920]{2,1,0:T(8,128)S(1)}, f32[3,5,1920]{2,1,0:T(8,128)S(1)}) custom-call(s32[3]{0:T(128)S(1)} %pad_add_fusion.1.me_ref, s32[32,3,120]{2,1,0:T(4,128)S(1)} %all-to-all-done.table_ref, f32[4,9,160,128]{3,2,1,0:T(8,128)S(1)} %copy-done.2, f32[1,3,16,1920]{3,2,1,0:T(8,128)S(1)} %copy-done), custom_call_target="tpu_custom_call" | custom-call | flops 192000000 | tf_op jit(solution)/shard_map/pallas_call | solution.py:582
  35.5 5.8 %all-to-all-start.1 = ((f32[32,40,128]{2,1,0:T(8,128)}), f32[32,40,128]{2,1,0:T(8,128)S(1)}, u32[]{:S(2)}, u32[]{:S(2)}) async-start(f32[32,40,128]{2,1,0:T(8,128)} %get-tuple-element.14), calls=%async_computation.1 | async-start | bytes 1310720 | tf_op jit(solution)/shard_map/all_to_all | solution.py:601
  41.3 3.7 %collective-permute-start = (f32[3,5,1920]{2,1,0:T(8,128)S(1)}, f32[3,5,1920]{2,1,0:T(8,128)S(1)}, u32[]{:S(2)}, u32[]{:S(2)}) collective-permute-start(f32[3,5,1920]{2,1,0:T(8,128)S(1)} %get-tuple-element.15), channel_id=1, source_target_pairs={{0,2},{2,4},{4,6},{8,10},{10,12},{12,14},{14,16},{16,18},{18,20},{... | collective-permute-start | bytes 345608 | tf_op jit(solution)/shard_map/ppermute | solution.py:599
  45.0 5.8 %collective-permute-start.1 = (f32[3,5,1920]{2,1,0:T(8,128)S(1)}, f32[3,5,1920]{2,1,0:T(8,128)S(1)}, u32[]{:S(2)}, u32[]{:S(2)}) collective-permute-start(f32[3,5,1920]{2,1,0:T(8,128)S(1)} %get-tuple-element.16), channel_id=1, source_target_pairs={{2,0},{4,2},{6,4},{10,8},{12,10},{14,12},{16,14},{18,16},{20,18},{... | collective-permute-start | bytes 345608 | tf_op jit(solution)/shard_map/ppermute | solution.py:600
  50.8 11.7 %collective-permute-done.up_ref.target_up = f32[3,5,1920]{2,1,0:T(8,128)S(1)} collective-permute-done((f32[3,5,1920]{2,1,0:T(8,128)S(1)}, f32[3,5,1920]{2,1,0:T(8,128)S(1)}, u32[]{:S(2)}, u32[]{:S(2)}) %collective-permute-start) | collective-permute-done | bytes 115232 | tf_op jit(solution)/shard_map/ppermute | solution.py:599
  62.5 0.0 collective-permute-done.1.down_ref.target_down
  62.5 3.5 %shard_map.79.fixed_ref = f32[2,3,16,1920]{3,2,1,0:T(8,128)S(1)} custom-call(f32[1,3,16,1920]{3,2,1,0:T(8,128)S(1)} %copy-done, f32[3,5,1920]{2,1,0:T(8,128)S(1)} %collective-permute-done.up_ref.target_up, f32[3,5,1920]{2,1,0:T(8,128)S(1)} %collective-permute-done.1.down_ref.target_down), custom_call_target="tpu_custom_call" | custom-call | flops 192000000 | tf_op jit(solution)/shard_map/pallas_call | solution.py:603
  66.0 0.0 all-to-all-done.1
  66.1 1.4 %shard_map.80 = f32[768,128]{1,0:T(8,128)S(1)} custom-call(s32[8,128]{1,0:T(8,128)S(1)} %get-tuple-element.13.route_ref, f32[1280,128]{1,0:T(8,128)S(1)} %bitcast.9, f32[2,3,16,1920]{3,2,1,0:T(8,128)S(1)} %shard_map.79.fixed_ref), custom_call_target="tpu_custom_call" | custom-call | tf_op jit(solution)/shard_map/pallas_call | solution.py:610
  67.4 16.9 %all_to_all.15.got_ref = f32[16,48,128]{2,1,0:T(8,128)S(1)} all-to-all(f32[16,48,128]{2,1,0:T(8,128)S(1)} %bitcast.10), channel_id=1, replica_groups=mesh['cell'=16,'view'=2] {'cell'}, dimensions={0} | all-to-all | bytes 786432 | tf_op jit(solution)/shard_map/all_to_all | solution.py:615
  84.3 1.6 %shard_map.81 = (f32[1,3,16,1920]{3,2,1,0:T(8,128)S(1)}, f32[3,5,1920]{2,1,0:T(8,128)S(1)}, f32[3,5,1920]{2,1,0:T(8,128)S(1)}) custom-call(s32[32,128]{1,0:T(8,128)S(1)} %get-tuple-element.12.code_ref, s32[3]{0:T(128)S(1)} %pad_add_fusion.1.me_ref, f32[16,48,128]{2,1,0:T(8,128)S(1)} %all_to_all.15.got_ref), custom_call_target="tpu_custom_call" | custom-call | tf_op jit(solution)/shard_map/pallas_call | solution.py:618
  85.9 2.5 %collective-permute-start.2 = (f32[3,5,1920]{2,1,0:T(8,128)S(1)}, f32[3,5,1920]{2,1,0:T(8,128)S(1)}, u32[]{:S(2)}, u32[]{:S(2)}) collective-permute-start(f32[3,5,1920]{2,1,0:T(8,128)S(1)} %get-tuple-element.18), channel_id=1, source_target_pairs={{0,2},{2,4},{4,6},{8,10},{10,12},{12,14},{14,16},{16,18},{18,20},{... | collective-permute-start | bytes 345608 | tf_op jit(solution)/shard_map/ppermute | solution.py:624
  88.4 7.0 %collective-permute-start.3 = (f32[3,5,1920]{2,1,0:T(8,128)S(1)}, f32[3,5,1920]{2,1,0:T(8,128)S(1)}, u32[]{:S(2)}, u32[]{:S(2)}) collective-permute-start(f32[3,5,1920]{2,1,0:T(8,128)S(1)} %get-tuple-element.19), channel_id=1, source_target_pairs={{2,0},{4,2},{6,4},{10,8},{12,10},{14,12},{16,14},{18,16},{20,18},{... | collective-permute-start | bytes 345608 | tf_op jit(solution)/shard_map/ppermute | solution.py:625
  95.4 4.7 %shard_map.82.own_ref = f32[3,3,16,1920]{3,2,1,0:T(8,128)S(1)} custom-call(f32[1,3,16,1920]{3,2,1,0:T(8,128)S(1)} %get-tuple-element.17.image_ref, f32[1,3,16,1920]{3,2,1,0:T(8,128)S(1)} %copy-done), custom_call_target="tpu_custom_call" | custom-call | flops 192000000 | tf_op jit(solution)/shard_map/pallas_call | solution.py:627
  100.1 0.0 collective-permute-done.2.up_ref
  100.1 0.0 collective-permute-done.3.down_ref
  100.1 5.2 %shard_map.83 = (f32[1,3,16,1920]{3,2,1,0:T(8,128)}, f32[1,16,1920]{2,1,0:T(8,128)}) custom-call(f32[1,3,16,1920]{3,2,1,0:T(8,128)S(1)} %get-tuple-element.17.image_ref, f32[1,3,16,1920]{3,2,1,0:T(8,128)S(1)} %copy-done, f32[3,3,16,1920]{3,2,1,0:T(8,128)S(1)} %shard_map.82.own_ref, f32[2,3,16,1920]{3,2,1,0:T(8,128)S(1)} %shard_map.79.fixed_ref, ...), custom_call_target="tpu_custom_call" | custom-call | tf_op jit(solution)/shard_map/pallas_call | solution.py:630
  (1 shorter events, 0.0 us)
Async XLA Ops:
  0.6 18.4 %copy-start = (f32[1,3,16,1920]{3,2,1,0:T(8,128)S(1)}, f32[1,3,16,1920]{3,2,1,0:T(8,128)}, u32[]{:S(2)}) copy-start(f32[1,3,16,1920]{3,2,1,0:T(8,128)} %target_ref.7) | copy-start | bytes 1105924
  2.0 17.0 %all-to-all-start = ((s32[32,3,120]{2,1,0:T(4,128)}), s32[32,3,120]{2,1,0:T(4,128)S(1)}, u32[]{:S(2)}, u32[]{:S(2)}) async-start(s32[32,3,120]{2,1,0:T(4,128)} %broadcast_in_dim.3), calls=%async_computation | async-start | bytes 131072 | tf_op jit(solution)/shard_map/all_to_all | solution.py:562
  9.3 1.0 copy-start.3
  10.3 0.7 copy-start.4
  17.4 1.6 %copy-start.1 = (f32[4,9,160,128]{3,2,1,0:T(8,128)}, f32[4,9,160,128]{3,2,1,0:T(8,128)S(1)}, u32[]{:S(2)}) copy-start(f32[4,9,160,128]{3,2,1,0:T(8,128)S(1)} %get-tuple-element.11.feats_ref) | copy-start | bytes 8847364
  19.0 1.8 %copy-start.2 = (f32[4,9,160,128]{3,2,1,0:T(8,128)S(1)}, f32[4,9,160,128]{3,2,1,0:T(8,128)}, u32[]{:S(2)}) copy-start(f32[4,9,160,128]{3,2,1,0:T(8,128)} %copy-done.1) | copy-start | bytes 8847364
  35.5 30.5 %all-to-all-start.1 = ((f32[32,40,128]{2,1,0:T(8,128)}), f32[32,40,128]{2,1,0:T(8,128)S(1)}, u32[]{:S(2)}, u32[]{:S(2)}) async-start(f32[32,40,128]{2,1,0:T(8,128)} %get-tuple-element.14), calls=%async_computation.1 | async-start | bytes 1310720 | tf_op jit(solution)/shard_map/all_to_all | solution.py:601
  41.3 21.2 %collective-permute-start = (f32[3,5,1920]{2,1,0:T(8,128)S(1)}, f32[3,5,1920]{2,1,0:T(8,128)S(1)}, u32[]{:S(2)}, u32[]{:S(2)}) collective-permute-start(f32[3,5,1920]{2,1,0:T(8,128)S(1)} %get-tuple-element.15), channel_id=1, source_target_pairs={{0,2},{2,4},{4,6},{8,10},{10,12},{12,14},{14,16},{16,18},{18,20},{... | collective-permute-start | bytes 345608 | tf_op jit(solution)/shard_map/ppermute | solution.py:599
  45.0 17.5 %collective-permute-start.1 = (f32[3,5,1920]{2,1,0:T(8,128)S(1)}, f32[3,5,1920]{2,1,0:T(8,128)S(1)}, u32[]{:S(2)}, u32[]{:S(2)}) collective-permute-start(f32[3,5,1920]{2,1,0:T(8,128)S(1)} %get-tuple-element.16), channel_id=1, source_target_pairs={{2,0},{4,2},{6,4},{10,8},{12,10},{14,12},{16,14},{18,16},{20,18},{... | collective-permute-start | bytes 345608 | tf_op jit(solution)/shard_map/ppermute | solution.py:600
  85.9 14.2 %collective-permute-start.2 = (f32[3,5,1920]{2,1,0:T(8,128)S(1)}, f32[3,5,1920]{2,1,0:T(8,128)S(1)}, u32[]{:S(2)}, u32[]{:S(2)}) collective-permute-start(f32[3,5,1920]{2,1,0:T(8,128)S(1)} %get-tuple-element.18), channel_id=1, source_target_pairs={{0,2},{2,4},{4,6},{8,10},{10,12},{12,14},{14,16},{16,18},{18,20},{... | collective-permute-start | bytes 345608 | tf_op jit(solution)/shard_map/ppermute | solution.py:624
  88.4 11.7 %collective-permute-start.3 = (f32[3,5,1920]{2,1,0:T(8,128)S(1)}, f32[3,5,1920]{2,1,0:T(8,128)S(1)}, u32[]{:S(2)}, u32[]{:S(2)}) collective-permute-start(f32[3,5,1920]{2,1,0:T(8,128)S(1)} %get-tuple-element.19), channel_id=1, source_target_pairs={{2,0},{4,2},{6,4},{10,8},{12,10},{14,12},{16,14},{18,16},{20,18},{... | collective-permute-start | bytes 345608 | tf_op jit(solution)/shard_map/ppermute | solution.py:625

commit v3 on v2

--- a/solution.py
+++ b/solution.py
@@ -27,7 +27,10 @@
     return whole, value - whole * size
 
 
-def own_route(cells, groups, blocks, cap, rcap, per_row, table_ref, route_ref, box):
+def route_kernel(
+    cells, blocks, cap, rcap, per_row, me_ref, table_ref, all_ref, late_ref, route_ref, code_ref, box, ids
+):
+    del late_ref
     length, tiles = table_ref.shape[0] - 1, table_ref.shape[1]
     box[...] = jnp.full(box.shape, -1.0, F32)
     box[0 : length + 1, 0:tiles] = table_ref[...].astype(F32)
@@ -50,12 +53,35 @@
         for m in range(n):
             rank = rank + count(owner == owner_rows[m])
         values.append(jnp.where(entry >= 0.0, owner * cap + rank, -1.0))
-    values.append(stripe * rcap + tile_rank)
+    message = 10 * rcap
+    lower = jnp.where(stripe + 1.0 < cells, stripe + 1.0, 0.0)
+    upper = jnp.where(stripe > 0.0, stripe - 1.0, cells - 1.0)
+    values.append(stripe * message + 6 * tile_rank)
+    values.append(lower * message + 6 * rcap + 2 * tile_rank)
+    values.append(upper * message + 8 * rcap + 2 * tile_rank)
     lane = iota((LANES, LANES), 1)
     route = jnp.zeros((LANES, LANES), F32)
     for number, value in enumerate(values):
         route = jnp.where(lane == number, value, route)
     route_ref[...] = route.T[0:8, :].astype(jnp.int32)
+
+    devices = all_ref.shape[0]
+    ids[...] = jnp.full(ids.shape, -1.0, F32)
+    ids[:, 0:tiles] = all_ref[:, length, :].astype(F32)
+    stripe, column = split(ids[...], per_row)
+    before = jnp.where(iota((LANES, LANES), 0) < iota((LANES, LANES), 1), 1.0, 0.0)
+    my_stripe = me_ref[1].astype(F32)
+    code_lane = iota((devices, LANES), 1)
+    codes = jnp.zeros((devices, LANES), F32)
+    lower = jnp.where(my_stripe + 1.0 < cells, my_stripe + 1.0, 0.0)
+    upper = jnp.where(my_stripe > 0.0, my_stripe - 1.0, cells - 1.0)
+    for number, wanted in enumerate((my_stripe, upper, lower)):
+        here = stripe == wanted
+        rank = jnp.dot(jnp.where(here, 1.0, 0.0), before, preferred_element_type=F32)
+        for k in range(rcap):
+            lane = number * rcap + k
+            codes = jnp.where(code_lane == lane, jnp.sum(jnp.where(here & (rank == k), column + 1.0, 0.0), axis=1, keepdims=True), codes)
+    code_ref[...] = codes.astype(jnp.int32)
 
 
 def harmonics(x, y, z):
@@ -143,9 +169,8 @@
 
 
 def prepare_kernel(
-    cells, groups, cap, rcap, per_row,
-    cams_ref, table_ref, params_hbm, seen_hbm, feats_ref, route_ref,
-    box, stage, seen_stage, params_ref, seen_ref, sems,
+    cams_ref, params_hbm, seen_hbm, feats_ref,
+    stage, seen_stage, params_ref, seen_ref, sems,
 ):
     features, total = params_ref.shape
     blocks = total // GBLK
@@ -162,7 +187,6 @@
             pltpu.make_async_copy(params_hbm.at[:, lanes], params_ref.at[:, lanes], sems.at[piece])
         )
         copies[-1].start()
-    own_route(cells, groups, blocks, cap, rcap, per_row, table_ref, route_ref, box)
     seen_copy.wait()
 
     def project_group(group):
@@ -190,12 +214,19 @@
 
 
 def render_kernel(
-    cells, groups, cap, rcap, per_row, blocks,
-    me_ref, table_ref, feats_ref, target_ref, out_ref, code_ref, head_ref, tail_ref,
-    box, info, turned, shades, rest, sheets, code_box, code_smem, sem,
+    cells, groups, cap, per_row, blocks,
+    me_ref, table_ref, feats_ref, target_ref, out_hbm, head_hbm, tail_hbm,
+    box, info, turned, shades, rest, sheets, code_box, code_smem, out_ref, edges, sems,
 ):
-    head_ref[...] = target_ref[0, :, 0:5, :]
-    tail_ref[...] = target_ref[0, :, 11:16, :]
+    edges[0] = target_ref[0, :, 0:5, :]
+    edges[1] = target_ref[0, :, 11:16, :]
+    outward = [
+        pltpu.make_async_copy(edges.at[0], head_hbm, sems.at[1]),
+        pltpu.make_async_copy(edges.at[1], tail_hbm, sems.at[2]),
+        pltpu.make_async_copy(out_ref, out_hbm, sems.at[3]),
+    ]
+    outward[0].start()
+    outward[1].start()
     devices = cells * groups
     quarter, half = cells // 4, cells // 2
     length, tiles = table_ref.shape[1] - 1, table_ref.shape[2]
@@ -204,7 +235,6 @@
     for n in range(length + 1):
         box[n, :, 0:tiles] = table_ref[:, n, :].astype(F32)
     me = me_ref[0].astype(F32)
-    my_stripe = me_ref[1].astype(F32)
     before = jnp.where(iota((LANES, LANES), 0) < iota((LANES, LANES), 1), 1.0, 0.0)
 
     def ranks(mask):
@@ -236,13 +266,8 @@
         tile = sum(pick(hit & (rank == k), tile_code) for hit, rank, local_slot in mine)
         codes = jnp.where(code_lane == k, asked, codes)
         found = found + jnp.sum(jnp.where(slot_lane == asked - 1.0, tile, 0.0), axis=0, keepdims=True)
-    here = stripe == my_stripe
-    rank, _ = ranks(here)
-    for k in range(rcap):
-        codes = jnp.where(code_lane == cap + k, pick(here & (rank == k), column + 1.0), codes)
     code_box[...] = codes.astype(jnp.int32)
-    code_ref[...] = codes.astype(jnp.int32)
-    scalars = pltpu.make_async_copy(code_box, code_smem, sem)
+    scalars = pltpu.make_async_copy(code_box, code_smem, sems.at[0])
     scalars.start()
 
     for part in range(2):
@@ -340,50 +365,44 @@
             place = jnp.clip(code_smem[d, k] - 1, 0, blocks - 1)
             out_ref[d, pl.ds(8 * k, 8), :] = sheets[pl.ds(pl.multiple_of(8 * place, 8), 8), :]
 
-
-def combine_kernel(tiles, route_ref, got_ref, fixed_ref, out_ref):
-    del fixed_ref
+    outward[2].start()
+    for copy in outward:
+        copy.wait()
+
+
+def lane_group(low, high):
+    group = iota((8, LANES), 1) >> 4
+    return (group >= low) & (group <= high)
+
+
+def combine_kernel(tiles, route_ref, got_ref, early_up, early_down, out_ref):
+    del early_up, early_down
     line = iota((8, LANES), 0)
+    from_half = ((line == 0) & lane_group(1, 3)) | ((line == 1) & (lane_group(6, 7) | lane_group(0, 0)))
+    from_left = ((line == 2) & lane_group(1, 1)) | ((line == 3) & lane_group(6, 6))
+    from_right = ((line == 2) & lane_group(3, 3)) | ((line == 3) & lane_group(0, 0))
 
     @pl.loop(0, tiles, unroll=8)
     def _(t):
         front = route_ref[0, t]
         back = route_ref[1, t]
-        where_to = route_ref[2, t]
         near = got_ref[pl.ds(pl.multiple_of(8 * front, 8), 8), :]
         far = got_ref[pl.ds(pl.multiple_of(8 * jnp.maximum(back, 0), 8), 8), :]
         keep = jnp.where(line >= 6, near, 0.0)
         keep = keep + pltpu.roll(keep, 4, 0)
         keep = keep + pltpu.roll(keep, 2, 0)
         tile = near + jnp.where(back >= 0, keep * far, 0.0)
-        out_ref[pl.ds(6 * where_to, 6), :] = tile[0:6, :]
-
-
-def place_kernel(
-    groups, cap, rcap, per_row, code_ref, me_ref, got_ref, image_ref, head_ref, tail_ref, board
-):
-    cells = got_ref.shape[0]
-
-    @pl.loop(0, cells)
-    def _(cell):
-        for k in range(rcap):
-            column = code_ref[cell * groups + me_ref[2], cap + k] - 1
-            spot = jnp.where(column < 0, per_row, column)
-            board[pl.ds(8 * spot, 6), :] = got_ref[cell, 6 * k : 6 * k + 6, :]
-
-    group = iota((8, LANES), 1) >> 4
-    masks = [jnp.bitwise_and(group, bit) != 0 for bit in (1, 2, 4)]
-    for j in range(per_row // 8):
-        for c in range(3):
-            for h in range(2):
-                made = board[pl.ds(64 * j + 2 * c + h, 8, stride=8), :]
-                made = pltpu.roll(made, 0, 1, stride=16, stride_axis=0)
-                for mask, bit in zip(masks, (1, 2, 4)):
-                    made = jnp.where(mask, pltpu.roll(made, 8 - bit, 0), made)
-                made = pltpu.roll(made, 0, 1, stride=16, stride_axis=0)
-                image_ref[0, c, 8 * h : 8 * h + 8, 128 * j : 128 * j + 128] = made
-    head_ref[...] = image_ref[0, :, 0:5, :]
-    tail_ref[...] = image_ref[0, :, 11:16, :]
+        out_ref[pl.ds(route_ref[2, t], 6), :] = tile[0:6, :]
+        two_up = pltpu.roll(tile, 6, 0)
+        edge = jnp.where(from_half, pltpu.roll(pltpu.roll(tile, 4, 0), 64, 1), tile)
+        edge = jnp.where(from_left, pltpu.roll(two_up, 16, 1), edge)
+        edge = jnp.where(from_right, pltpu.roll(two_up, LANES - 16, 1), edge)
+        low = route_ref[3, t]
+        high = route_ref[4, t]
+        out_ref[pl.ds(low, 1), :] = edge[1:2, :]
+        out_ref[pl.ds(low + 1, 1), :] = edge[3:4, :]
+        out_ref[pl.ds(high, 1), :] = edge[0:1, :]
+        out_ref[pl.ds(high + 1, 1), :] = edge[2:3, :]
 
 
 def window_taps():
@@ -392,12 +411,12 @@
     return [value / whole for value in raw]
 
 
-def across_rows(tall, first, count):
+def across_rows(tall, rows, first, count):
     taps = window_taps()
     around = (count + 2) * LANES
     blurred = []
     for f in range(tall.shape[0]):
-        given = tall[f, :, LANES * first : LANES * first + around]
+        given = tall[f, rows, LANES * first : LANES * first + around]
         near = [pltpu.roll(given, 1, 1), given, pltpu.roll(given, around - 1, 1), pltpu.roll(given, around - 2, 1)]
         far = []
         for a in range(3):
@@ -418,11 +437,11 @@
     tall[:, :, tall.shape[2] - LANES :] = blank
 
 
-def down_columns(fields, f):
+def down_columns(fields, u, f):
     taps = window_taps()
-    total = taps[0] * fields[f, 5:21, :]
+    total = taps[0] * fields[u, f, 8:24, :]
     for k in range(1, 6):
-        total = total + taps[k] * (fields[f, 5 - k : 21 - k, :] + fields[f, 5 + k : 21 + k, :])
+        total = total + taps[k] * (fields[u, f, 8 - k : 24 - k, :] + fields[u, f, 8 + k : 24 + k, :])
     return total
 
 
@@ -431,106 +450,132 @@
 
 
 RUN = 5
-
-
-def target_kernel(target_ref, up_ref, down_ref, out_ref, fields, tall):
+HALVES = (slice(0, 8), slice(8, 16))
+
+
+def target_kernel(target_ref, up_ref, down_ref, late_ref, out_ref, fields, tall):
+    del late_ref
     spans = target_ref.shape[3] // LANES
     clear_sides(tall)
 
     @pl.loop(0, 3)
     def _(c):
-        @pl.loop(0, spans)
-        def _(j):
-            fields[0, 0:5, :] = up_ref[c, :, span(j)]
-            fields[0, 5:21, :] = target_ref[0, c, :, span(j)]
-            fields[0, 21:26, :] = down_ref[c, :, span(j)]
-            fields[1] = fields[0] * fields[0]
-            for f in range(2):
-                tall[f, :, span(j + 1)] = down_columns(fields, f)
+        @pl.loop(0, spans // RUN)
+        def _(run):
+            for u in range(RUN):
+                j = RUN * run + u
+                for low, high, y in (
+                    (3, 8, up_ref[c, :, span(j)]),
+                    (8, 24, target_ref[0, c, :, span(j)]),
+                    (24, 29, down_ref[c, :, span(j)]),
+                ):
+                    fields[u, 0, low:high, :] = y
+                    fields[u, 1, low:high, :] = y * y
+            for u in range(RUN):
+                for f in range(2):
+                    tall[f, :, span(RUN * run + u + 1)] = down_columns(fields, u, f)
 
         for first in range(0, spans, RUN):
-            count = min(RUN, spans - first)
-            for f, value in enumerate(across_rows(tall, first, count)):
-                out_ref[f, c, :, LANES * first : LANES * (first + count)] = value
-
-
-def own_kernel(image_ref, target_ref, out_ref, fields, tall):
+            count = RUN
+            for rows in HALVES:
+                for f, value in enumerate(across_rows(tall, rows, first, count)):
+                    out_ref[f, c, rows, LANES * first : LANES * (first + count)] = value
+
+
+def finish_kernel(
+    groups, rcap, per_row,
+    code_ref, me_ref, got_ref, target_ref, fixed_ref, target_up, target_down, image_ref, loss_ref,
+    board, edges, halo, fields, tall,
+):
+    cells = got_ref.shape[0]
     spans = target_ref.shape[3] // LANES
+
+    @pl.loop(0, cells)
+    def _(cell):
+        line = cell * groups + me_ref[2]
+
+        def spot(k):
+            column = code_ref[line, k] - 1
+            return jnp.where(column < 0, per_row, column)
+
+        for k in range(rcap):
+            board[pl.ds(8 * spot(k), 6), :] = got_ref[cell, 6 * k : 6 * k + 6, :]
+        for side in range(2):
+            for k in range(rcap):
+                first = (6 + 2 * side) * rcap + 2 * k
+                edges[side, pl.ds(2 * spot((1 + side) * rcap + k), 2), :] = got_ref[cell, first : first + 2, :]
+
+    masks = [jnp.bitwise_and(iota((8, LANES), 1) >> 4, bit) != 0 for bit in (1, 2, 4)]
+
+    def pixels(made):
+        made = pltpu.roll(made, 0, 1, stride=16, stride_axis=0)
+        for mask, bit in zip(masks, (1, 2, 4)):
+            made = jnp.where(mask, pltpu.roll(made, 8 - bit, 0), made)
+        return pltpu.roll(made, 0, 1, stride=16, stride_axis=0)
+
+    for j in range(spans):
+        lanes = slice(LANES * j, LANES * j + LANES)
+        for c in range(3):
+            for h in range(2):
+                image_ref[0, c, 8 * h : 8 * h + 8, lanes] = pixels(
+                    board[pl.ds(64 * j + 2 * c + h, 8, stride=8), :]
+                )
+        for side in range(2):
+            kept = me_ref[3 + side] > 0
+            first = edges[side, pl.ds(16 * j, 8, stride=2), :]
+            second = edges[side, pl.ds(16 * j + 1, 8, stride=2), :]
+            half = pltpu.roll(first, 64, 1)
+            left = pltpu.roll(second, LANES - 16, 1)
+            right = pltpu.roll(second, 16, 1)
+            if side == 0:
+                third = jnp.where(lane_group(2, 4), half, jnp.where(lane_group(1, 1), right, left))
+            else:
+                third = jnp.where(lane_group(5, 7), half, jnp.where(lane_group(4, 4), right, left))
+            for c, value in enumerate((first, second, third)):
+                halo[side, c, :, lanes] = jnp.where(kept, pixels(value), 0.0)
+
     clear_sides(tall)
-    fields[...] = jnp.zeros(fields.shape, F32)
 
     @pl.loop(0, 3)
     def _(c):
-        @pl.loop(0, spans)
-        def _(j):
-            x = image_ref[0, c, :, span(j)]
-            y = target_ref[0, c, :, span(j)]
-            fields[0, 5:21, :] = x
-            fields[1, 5:21, :] = x * x
-            fields[2, 5:21, :] = x * y
-            for f in range(3):
-                tall[f, :, span(j + 1)] = down_columns(fields, f)
+        @pl.loop(0, spans // RUN)
+        def _(run):
+            for u in range(RUN):
+                j = RUN * run + u
+                for low, high, x, y in (
+                    (3, 8, halo[0, c, 3:8, span(j)], target_up[c, :, span(j)]),
+                    (8, 24, image_ref[0, c, :, span(j)], target_ref[0, c, :, span(j)]),
+                    (24, 29, halo[1, c, 0:5, span(j)], target_down[c, :, span(j)]),
+                ):
+                    fields[u, 0, low:high, :] = x
+                    fields[u, 1, low:high, :] = x * x
+                    fields[u, 2, low:high, :] = x * y
+            for u in range(RUN):
+                for f in range(3):
+                    tall[f, :, span(RUN * run + u + 1)] = down_columns(fields, u, f)
 
         for first in range(0, spans, RUN):
-            count = min(RUN, spans - first)
-            for f, value in enumerate(across_rows(tall, first, count)):
-                out_ref[f, c, :, LANES * first : LANES * (first + count)] = value
-
-
-def loss_kernel(
-    image_ref, target_ref, own_ref, fixed_ref, up_ref, down_ref, target_up, target_down,
-    image_out, loss_ref, fields, tall,
-):
-    taps = window_taps()
-    image_out[...] = image_ref[...]
-    spans = image_ref.shape[3] // LANES
-    clear_sides(tall)
-    fields[...] = jnp.zeros(fields.shape, F32)
-
-    @pl.loop(0, 3)
-    def _(c):
-        @pl.loop(0, spans)
-        def _(j):
-            x = up_ref[c, :, span(j)]
-            y = target_up[c, :, span(j)]
-            for f, value in enumerate((x, x * x, x * y)):
-                fields[f, 3:8, :] = value
-            x = down_ref[c, :, span(j)]
-            y = target_down[c, :, span(j)]
-            for f, value in enumerate((x, x * x, x * y)):
-                fields[f, 24:29, :] = value
-            for f in range(3):
-                above = taps[1] * fields[f, 7:15, :]
-                below = taps[1] * fields[f, 17:25, :]
-                for k in range(2, 6):
-                    above = above + taps[k] * fields[f, 8 - k : 16 - k, :]
-                    below = below + taps[k] * fields[f, 16 + k : 24 + k, :]
-                tall[f, 0:8, span(j + 1)] = above
-                tall[f, 8:16, span(j + 1)] = below
-
-        for first in range(0, spans, RUN):
-            count = min(RUN, spans - first)
+            count = RUN
             lanes = slice(LANES * first, LANES * (first + count))
-            mx, xx, xy = [
-                value + own_ref[f, c, :, lanes]
-                for f, value in enumerate(across_rows(tall, first, count))
-            ]
-            my = fixed_ref[0, c, :, lanes]
-            both = mx * my
-            sums = mx * mx + my * my
-            ssim = (2.0 * both + 0.0001) * (2.0 * (xy - both) + 0.0009) / (
-                (sums + 0.0001) * (xx + fixed_ref[1, c, :, lanes] - sums + 0.0009)
-            )
-            gap = jnp.abs(image_ref[0, c, :, lanes] - target_ref[0, c, :, lanes])
-            part = (0.8 / 3.0) * gap - (0.2 / 3.0) * ssim
-            loss_ref[0, :, lanes] = jnp.where(c == 0, 0.2, loss_ref[0, :, lanes]) + part
-
-
-def call(kernel, outs, specs, scratch=(), mem=8, work=0):
+            for rows in HALVES:
+                mx, xx, xy = across_rows(tall, rows, first, count)
+                my = fixed_ref[0, c, rows, lanes]
+                both = mx * my
+                sums = mx * mx + my * my
+                ssim = (2.0 * both + 0.0001) * (2.0 * (xy - both) + 0.0009) / (
+                    (sums + 0.0001) * (xx + fixed_ref[1, c, rows, lanes] - sums + 0.0009)
+                )
+                gap = jnp.abs(image_ref[0, c, rows, lanes] - target_ref[0, c, rows, lanes])
+                part = (0.8 / 3.0) * gap - (0.2 / 3.0) * ssim
+                loss_ref[0, rows, lanes] = jnp.where(c == 0, 0.2, loss_ref[0, rows, lanes]) + part
+
+
+def call(kernel, outs, specs, scratch=(), mem=8, work=0, out_space=VMEM):
     return pl.pallas_call(
         kernel,
         out_shape=outs,
         in_specs=[pl.BlockSpec(memory_space=spec) for spec in specs],
+        out_specs=jax.tree.map(lambda _: pl.BlockSpec(memory_space=out_space), outs),
         scratch_shapes=list(scratch),
         cost_estimate=pl.CostEstimate(flops=work, bytes_accessed=0, transcendentals=0) if work else None,
         compiler_params=pltpu.CompilerParams(vmem_limit_bytes=mem * 2**20),
@@ -554,7 +599,11 @@
     shape = jax.ShapeDtypeStruct
     my_cell = lax.axis_index("cell").astype(jnp.int32)
     my_view = lax.axis_index("view").astype(jnp.int32)
-    me = jnp.stack([my_cell * groups + my_view, my_cell, my_view])
+    place = (my_cell + (cells - quarter)) % half
+    me = jnp.stack(
+        [my_cell * groups + my_view, my_cell, my_view]
+        + [(place != edge).astype(jnp.int32) for edge in (0, half - 1)]
+    )
     down_pairs = [(s, (s + 1) % cells) for s in range(cells) if (s - quarter) % half != half - 1]
     up_pairs = [(b, a) for a, b in down_pairs]
     lists = jnp.swapaxes(tile_blocks[0, 0], 0, 1)
@@ -564,12 +613,11 @@
         ("cell", "view"), split_axis=0, concat_axis=0, tiled=True,
     )
     work = blocks * GBLK * 10000
-    feats, route = call(
-        functools.partial(prepare_kernel, cells, groups, cap, rcap, per_row),
-        (shape((visible.shape[0], 9, rows, GBLK), F32), shape((8, LANES), jnp.int32)),
-        [SMEM, VMEM, HBM, HBM],
+    feats = call(
+        prepare_kernel,
+        shape((visible.shape[0], 9, rows, GBLK), F32),
+        [SMEM, HBM, HBM],
         [
-            VMEM((LANES, LANES), F32),
             VMEM((512, LANES), F32),
             VMEM((64, LANES), jnp.int32),
             VMEM(gauss_params.shape, F32),
@@ -577,11 +625,11 @@
             pltpu.SemaphoreType.DMA((PIECES + 1,)),
         ],
         50, work,
-    )(cameras, own_table, gauss_params, visible)
+    )(cameras, gauss_params, visible)
     edge = shape((3, 5, width), F32)
-    made, code, target_head, target_tail = call(
-        functools.partial(render_kernel, cells, groups, cap, rcap, per_row, blocks),
-        (shape((devices, 8 * cap, LANES), F32), shape((devices, LANES), jnp.int32), edge, edge),
+    made, target_head, target_tail = call(
+        functools.partial(render_kernel, cells, groups, cap, per_row, blocks),
+        (HBM((devices, 8 * cap, LANES), F32), HBM(edge.shape, F32), HBM(edge.shape, F32)),
         [SMEM, VMEM, VMEM, VMEM],
         [
             VMEM((length + 1, devices, LANES), F32),
@@ -592,44 +640,51 @@
             VMEM((rows * 8, LANES), F32),
             VMEM((devices, LANES), jnp.int32),
             SMEM((devices, LANES), jnp.int32),
-            pltpu.SemaphoreType.DMA,
+            VMEM((devices, 8 * cap, LANES), F32),
+            VMEM((2,) + edge.shape, F32),
+            pltpu.SemaphoreType.DMA((4,)),
         ],
-        12, work,
+        12, work, HBM,
     )(me, table, feats, target)
     target_up = lax.ppermute(target_tail, "cell", down_pairs)
     target_down = lax.ppermute(target_head, "cell", up_pairs)
     got = lax.all_to_all(made, ("cell", "view"), split_axis=0, concat_axis=0, tiled=True)
     planes = shape((1, 3, 16, width), F32)
+    route, code = call(
+        functools.partial(route_kernel, cells, blocks, cap, rcap, per_row),
+        (shape((8, LANES), jnp.int32), shape((devices, LANES), jnp.int32)),
+        [SMEM, VMEM, VMEM, pl.ANY],
+        [VMEM((LANES, LANES), F32), VMEM((devices, LANES), F32)],
+        8, work,
+    )(me, own_table, table, target_head)
+    tile_rows = call(
+        functools.partial(combine_kernel, tiles),
+        shape((cells * 10 * rcap, LANES), F32),
+        [SMEM, VMEM, pl.ANY, pl.ANY],
+    )(route, got.reshape(devices * cap * 8, LANES), target_up, target_down)
+    got_tiles = lax.all_to_all(
+        tile_rows.reshape(cells, 10 * rcap, LANES), "cell", split_axis=0, concat_axis=0, tiled=True
+    )
     fixed = call(
         target_kernel,
         shape((2, 3, 16, width), F32),
-        [VMEM] * 3,
-        [VMEM((2, 32, LANES), F32), VMEM((2, 16, width + 2 * LANES), F32)],
+        [VMEM] * 3 + [pl.ANY],
+        [VMEM((RUN, 2, 32, LANES), F32), VMEM((2, 16, width + 2 * LANES), F32)],
         8, work,
-    )(target, target_up, target_down)
-    tile_rows = call(
-        functools.partial(combine_kernel, tiles),
-        shape((cells * 6 * rcap, LANES), F32),
-        [SMEM, VMEM, pl.ANY],
-    )(route, got.reshape(devices * cap * 8, LANES), fixed)
-    got_tiles = lax.all_to_all(
-        tile_rows.reshape(cells, 6 * rcap, LANES), "cell", split_axis=0, concat_axis=0, tiled=True
-    )
-    image, head, tail = call(
-        functools.partial(place_kernel, groups, cap, rcap, per_row),
-        (planes, edge, edge),
-        [SMEM, SMEM, VMEM],
-        [VMEM((8 * (per_row + 1), LANES), F32)],
-    )(code, me, got_tiles)
-    up_rows = lax.ppermute(tail, "cell", down_pairs)
-    down_rows = lax.ppermute(head, "cell", up_pairs)
-    blur_room = [VMEM((3, 32, LANES), F32), VMEM((3, 16, width + 2 * LANES), F32)]
-    own = call(
-        own_kernel, shape((3, 3, 16, width), F32), [VMEM] * 2, blur_room, 8, work
-    )(image, target)
+    )(target, target_up, target_down, tile_rows)
     return call(
-        loss_kernel, (planes, shape((1, 16, width), F32)), [VMEM] * 8, blur_room, 8
-    )(image, target, own, fixed, up_rows, down_rows, target_up, target_down)
+        functools.partial(finish_kernel, groups, rcap, per_row),
+        (planes, shape((1, 16, width), F32)),
+        [SMEM, SMEM] + [VMEM] * 5,
+        [
+            VMEM((8 * (per_row + 1), LANES), F32),
+            VMEM((2, 2 * (per_row + 4), LANES), F32),
+            VMEM((2, 3, 8, width), F32),
+            VMEM((RUN, 3, 32, LANES), F32),
+            VMEM((3, 16, width + 2 * LANES), F32),
+        ],
+        8,
+    )(code, me, got_tiles, target, fixed, target_up, target_down)
 
 
 def solution(mesh):

time: 106 us -> 96 us (0.906)
  blocking collectives: 16.9 us -> 0 us
  waiting for transfers between devices: 11.8 us -> 23.9 us
  starting transfers between devices: 32 us -> 26.3 us
  Pallas kernels: 37.3 us -> 40.5 us
  local copies, waits for them, and re-layouts: 5.7 us -> 3.3 us
    all_to_all x1 -> x0, blocking collectives: 16.9 us -> none  [local(): lax.all_to_all(tile_rows.reshape(cells, 6 * rcap, LANES), 'cell', split_a...]
    all_to_all x0 -> x1, waiting for transfers between devices: none -> 13.6 us  [local(): lax.all_to_all(tile_rows.reshape(cells, 10 * rcap, LANES), 'cell', split_...]
    ppermute x2 -> x0, starting transfers between devices: 9.43 us -> none  [the longest x1 6.97 us: local(): down_rows = lax.ppermute(head, 'cell', up_pairs)]
    all_to_all x0 -> x1, starting transfers between devices: none -> 3.73 us  [local(): lax.all_to_all(tile_rows.reshape(cells, 10 * rcap, LANES), 'cell', split_...]
    pallas_call x7 -> x6, Pallas kernels: 37.3 us -> 40.5 us  [the longest x1 14.6 us: local(): call(functools.partial(render_kernel, cells, groups, cap, per_row, blocks...]
    unnamed x10 -> x8, local copies, waits for them, and re-layouts: 5.06 us -> 2.58 us
    ppermute x1, waiting for transfers between devices: 11.7 us -> 9.59 us  [local(): target_up = lax.ppermute(target_tail, 'cell', down_pairs)]
  transfers between devices with their start and end apart: 6 -> 5, of which waited for: 1 -> 3; matrix products, arithmetic and copies ran while one was open for 0% -> 0% of each run, Pallas kernels for 14% -> 12%
where the time goes in v3:
time: 96 us; the launch traced here: 95.5 us
  Pallas kernels  40.5 us (42%)
  starting transfers between devices  26.3 us (27%)
  waiting for transfers between devices  23.9 us (25%)
  local copies, waits for them, and re-layouts  3.3 us (3%)
    pallas_call x1, Pallas kernels, local(): call(functools.partial(render_kernel, cells, groups, cap, per_row, blocks...  14.6 us
    all_to_all x1, waiting for transfers between devices, local(): lax.all_to_all(tile_rows.reshape(cells, 10 * rcap, LANES), 'cell', split_...  13.6 us
    pallas_call x1, Pallas kernels, local(): call(functools.partial(finish_kernel, groups, rcap, per_row), (planes, sh...  11.1 us
    ppermute x1, waiting for transfers between devices, local(): target_up = lax.ppermute(target_tail, 'cell', down_pairs)  9.59 us
    all_to_all x1, starting transfers between devices, local(): lax.all_to_all(jnp.broadcast_to(own_table, (devices, length + 1, tiles)),...  7.3 us
    pallas_call x1, Pallas kernels, local(): call(prepare_kernel, shape((visible.shape[0], 9, rows, GBLK), F32), [SMEM...  6.37 us
    all_to_all x1, starting transfers between devices, local(): lax.all_to_all(made, ('cell', 'view'), split_axis=0, concat_axis=0, tiled...  5.84 us
    ppermute x1, starting transfers between devices, local(): target_down = lax.ppermute(target_head, 'cell', up_pairs)  5.76 us
  transfers between devices with their start and end apart: 5, of which 3 were waited for; matrix products, arithmetic and copies ran while one was open for 0% of the time, Pallas kernels for 12%

profile of v3, /device:TPU:0, one launch (start us, length us, event | category | flops | bytes accessed | tf_op | source)
XLA Modules:
  0.0 95.5 jit_solution(9839598710944362761)
XLA Ops:
  0.6 0.0 copy-start
  0.6 0.8 pad_add_fusion.table_ref
  1.4 0.6 broadcast_in_dim.3
  2.0 7.3 %all-to-all-start = ((s32[32,3,120]{2,1,0:T(4,128)}), s32[32,3,120]{2,1,0:T(4,128)S(1)}, u32[]{:S(2)}, u32[]{:S(2)}) async-start(s32[32,3,120]{2,1,0:T(4,128)} %broadcast_in_dim.3), calls=%async_computation | async-start | bytes 131072 | tf_op jit(solution)/shard_map/all_to_all | solution.py:611
  9.4 0.1 stack.31.me_ref
  9.4 0.0 copy-start.1
  9.4 1.0 %copy-done.1 = s32[4,19200]{1,0:T(4,128)S(1)} copy-done((s32[4,19200]{1,0:T(4,128)S(1)}, s32[4,19200]{1,0:T(4,128)}, u32[]{:S(2)}) %copy-start.1) | copy-done | bytes 307224
  10.4 0.0 copy-start.2
  10.4 0.7 copy-done.2
  11.1 6.4 %shard_map.77.feats_ref = f32[4,9,160,128]{3,2,1,0:T(8,128)S(1)} custom-call(f32[4,15]{1,0:T(4,128)S(1)} %copy-done.2, f32[59,19200]{1,0:T(8,128)} %params_hbm.1, s32[4,19200]{1,0:T(4,128)S(1)} %copy-done.1), custom_call_target="tpu_custom_call" | custom-call | flops 192000000 | tf_op jit(solution)/shard_map/pallas_call | solution.py:616
  17.5 0.0 all-to-all-done.table_ref.all_ref
  17.5 0.0 copy-done
  17.5 14.6 %shard_map.78 = (f32[32,40,128]{2,1,0:T(8,128)}, f32[3,5,1920]{2,1,0:T(8,128)}, f32[3,5,1920]{2,1,0:T(8,128)}) custom-call(s32[5]{0:T(128)S(1)} %stack.31.me_ref, s32[32,3,120]{2,1,0:T(4,128)S(1)} %all-to-all-done.table_ref.all_ref, f32[4,9,160,128]{3,2,1,0:T(8,128)S(1)} %shard_map.77.feats_ref, f32[1,3,16,1920]{3,2,1,0:T(8,128)S(1)} %copy-done), custom_call_target="tpu_custom_call" | custom-call | flops 192000000 | tf_op jit(solution)/shard_map/pallas_call | solution.py:630
  32.1 5.8 %all-to-all-start.1 = ((f32[32,40,128]{2,1,0:T(8,128)}), f32[32,40,128]{2,1,0:T(8,128)S(1)}, u32[]{:S(2)}, u32[]{:S(2)}) async-start(f32[32,40,128]{2,1,0:T(8,128)} %get-tuple-element.10), calls=%async_computation.1 | async-start | bytes 1310720 | tf_op jit(solution)/shard_map/all_to_all | solution.py:651
  38.0 3.7 %collective-permute-start = (f32[3,5,1920]{2,1,0:T(8,128)}, f32[3,5,1920]{2,1,0:T(8,128)S(1)}, u32[]{:S(2)}, u32[]{:S(2)}) collective-permute-start(f32[3,5,1920]{2,1,0:T(8,128)} %get-tuple-element.11), channel_id=1, source_target_pairs={{0,2},{2,4},{4,6},{8,10},{10,12},{12,14},{14,16},{16,18},{18,20},{... | collective-permute-start | bytes 345608 | tf_op jit(solution)/shard_map/ppermute | solution.py:649
  41.6 5.8 %collective-permute-start.1 = (f32[3,5,1920]{2,1,0:T(8,128)}, f32[3,5,1920]{2,1,0:T(8,128)S(1)}, u32[]{:S(2)}, u32[]{:S(2)}) collective-permute-start(f32[3,5,1920]{2,1,0:T(8,128)} %get-tuple-element.7.late_ref), channel_id=1, source_target_pairs={{2,0},{4,2},{6,4},{10,8},{12,10},{14,12},{16,14},{18,16},{20,18},{... | collective-permute-start | bytes 345608 | tf_op jit(solution)/shard_map/ppermute | solution.py:650
  47.4 0.0 copy-start.3
  47.4 0.9 copy-done.3
  48.3 1.2 %shard_map.79 = (s32[8,128]{1,0:T(8,128)S(1)}, s32[32,128]{1,0:T(8,128)S(1)}) custom-call(s32[5]{0:T(128)S(1)} %stack.31.me_ref, s32[3,120]{1,0:T(4,128)S(1)} %pad_add_fusion.table_ref, s32[32,3,120]{2,1,0:T(4,128)S(1)} %all-to-all-done.table_ref.all_ref, f32[3,5,1920]{2,1,0:T(8,128)S(1)} %copy-done.3), custom_call_target="tpu_custom_call" | custom-call | flops 192000000 | tf_op jit(solution)/shard_map/pallas_call | solution.py:653
  49.6 9.6 %collective-permute-done.early_up.up_ref.target_up = f32[3,5,1920]{2,1,0:T(8,128)S(1)} collective-permute-done((f32[3,5,1920]{2,1,0:T(8,128)}, f32[3,5,1920]{2,1,0:T(8,128)S(1)}, u32[]{:S(2)}, u32[]{:S(2)}) %collective-permute-start) | collective-permute-done | bytes 115232 | tf_op jit(solution)/shard_map/ppermute | solution.py:649
  59.2 0.0 collective-permute-done.1.early_down.down_ref.target_down
  59.2 0.7 all-to-all-done.1
  59.8 3.4 %shard_map.80.late_ref = f32[1280,128]{1,0:T(8,128)} custom-call(s32[8,128]{1,0:T(8,128)S(1)} %get-tuple-element.9.route_ref, f32[1280,128]{1,0:T(8,128)S(1)} %bitcast.11, f32[3,5,1920]{2,1,0:T(8,128)S(1)} %collective-permute-done.early_up.up_ref.target_up, f32[3,5,1920]{2,1,0:T(8,128)S(1)} %collective-permute-done.1.early_down.down_ref.target_down), custom_call_target="tpu_custom_call" | custom-call | tf_op jit(solution)/shard_map/pallas_call | solution.py:660
  63.2 3.7 %all-to-all-start.2 = ((f32[16,80,128]{2,1,0:T(8,128)}), f32[16,80,128]{2,1,0:T(8,128)S(1)}, u32[]{:S(2)}, u32[]{:S(2)}) async-start(f32[16,80,128]{2,1,0:T(8,128)} %bitcast.9), calls=%async_computation.2 | async-start | bytes 1310720 | tf_op jit(solution)/shard_map/all_to_all | solution.py:665
  66.9 3.9 %shard_map.81.fixed_ref = f32[2,3,16,1920]{3,2,1,0:T(8,128)S(1)} custom-call(f32[1,3,16,1920]{3,2,1,0:T(8,128)S(1)} %copy-done, f32[3,5,1920]{2,1,0:T(8,128)S(1)} %collective-permute-done.early_up.up_ref.target_up, f32[3,5,1920]{2,1,0:T(8,128)S(1)} %collective-permute-done.1.early_down.down_ref.target_down, f32[1280,128]{1,0:T(8,128)} %shard_map.80.late_ref), custom_call_target="tpu_custom_call" | custom-call | flops 192000000 | tf_op jit(solution)/shard_map/pallas_call | solution.py:668
  70.8 13.6 %all-to-all-done.2.got_ref = f32[16,80,128]{2,1,0:T(8,128)S(1)} async-done(((f32[16,80,128]{2,1,0:T(8,128)}), f32[16,80,128]{2,1,0:T(8,128)S(1)}, u32[]{:S(2)}, u32[]{:S(2)}) %all-to-all-start.2) | async-done | bytes 655392 | tf_op jit(solution)/shard_map/all_to_all | solution.py:665
  84.4 11.1 %shard_map.82 = (f32[1,3,16,1920]{3,2,1,0:T(8,128)}, f32[1,16,1920]{2,1,0:T(8,128)}) custom-call(s32[32,128]{1,0:T(8,128)S(1)} %get-tuple-element.8.code_ref, s32[5]{0:T(128)S(1)} %stack.31.me_ref, f32[16,80,128]{2,1,0:T(8,128)S(1)} %all-to-all-done.2.got_ref, f32[1,3,16,1920]{3,2,1,0:T(8,128)S(1)} %copy-done, f32[2,3,16,1920]{3,2,1,0:T(8,128)S(1)} %shard_map.81.fixed_ref, ...), custom_call_target="tpu_custom_call" | custom-call | tf_op jit(solution)/shard_map/pallas_call | solution.py:675
Async XLA Ops:
  0.6 16.8 %copy-start = (f32[1,3,16,1920]{3,2,1,0:T(8,128)S(1)}, f32[1,3,16,1920]{3,2,1,0:T(8,128)}, u32[]{:S(2)}) copy-start(f32[1,3,16,1920]{3,2,1,0:T(8,128)} %target_ref.5) | copy-start | bytes 1105924
  2.0 15.4 %all-to-all-start = ((s32[32,3,120]{2,1,0:T(4,128)}), s32[32,3,120]{2,1,0:T(4,128)S(1)}, u32[]{:S(2)}, u32[]{:S(2)}) async-start(s32[32,3,120]{2,1,0:T(4,128)} %broadcast_in_dim.3), calls=%async_computation | async-start | bytes 131072 | tf_op jit(solution)/shard_map/all_to_all | solution.py:611
  9.4 1.0 %copy-start.1 = (s32[4,19200]{1,0:T(4,128)S(1)}, s32[4,19200]{1,0:T(4,128)}, u32[]{:S(2)}) copy-start(s32[4,19200]{1,0:T(4,128)} %seen_hbm.1) | copy-start | bytes 921604
  10.4 0.7 copy-start.2
  32.1 27.7 %all-to-all-start.1 = ((f32[32,40,128]{2,1,0:T(8,128)}), f32[32,40,128]{2,1,0:T(8,128)S(1)}, u32[]{:S(2)}, u32[]{:S(2)}) async-start(f32[32,40,128]{2,1,0:T(8,128)} %get-tuple-element.10), calls=%async_computation.1 | async-start | bytes 1310720 | tf_op jit(solution)/shard_map/all_to_all | solution.py:651
  38.0 21.2 %collective-permute-start = (f32[3,5,1920]{2,1,0:T(8,128)}, f32[3,5,1920]{2,1,0:T(8,128)S(1)}, u32[]{:S(2)}, u32[]{:S(2)}) collective-permute-start(f32[3,5,1920]{2,1,0:T(8,128)} %get-tuple-element.11), channel_id=1, source_target_pairs={{0,2},{2,4},{4,6},{8,10},{10,12},{12,14},{14,16},{16,18},{18,20},{... | collective-permute-start | bytes 345608 | tf_op jit(solution)/shard_map/ppermute | solution.py:649
  41.6 17.5 %collective-permute-start.1 = (f32[3,5,1920]{2,1,0:T(8,128)}, f32[3,5,1920]{2,1,0:T(8,128)S(1)}, u32[]{:S(2)}, u32[]{:S(2)}) collective-permute-start(f32[3,5,1920]{2,1,0:T(8,128)} %get-tuple-element.7.late_ref), channel_id=1, source_target_pairs={{2,0},{4,2},{6,4},{10,8},{12,10},{14,12},{16,14},{18,16},{20,18},{... | collective-permute-start | bytes 345608 | tf_op jit(solution)/shard_map/ppermute | solution.py:650
  47.4 0.9 copy-start.3
  63.2 21.2 %all-to-all-start.2 = ((f32[16,80,128]{2,1,0:T(8,128)}), f32[16,80,128]{2,1,0:T(8,128)S(1)}, u32[]{:S(2)}, u32[]{:S(2)}) async-start(f32[16,80,128]{2,1,0:T(8,128)} %bitcast.9), calls=%async_computation.2 | async-start | bytes 1310720 | tf_op jit(solution)/shard_map/all_to_all | solution.py:665

commit v4 on v3

--- a/solution.py
+++ b/solution.py
@@ -28,12 +28,12 @@
 
 
 def route_kernel(
-    cells, blocks, cap, rcap, per_row, me_ref, table_ref, all_ref, late_ref, route_ref, code_ref, box, ids
+    cells, blocks, cap, rcap, per_row, me_ref, all_ref, late_ref, route_ref, code_ref, box, ids
 ):
     del late_ref
-    length, tiles = table_ref.shape[0] - 1, table_ref.shape[1]
+    length, tiles = all_ref.shape[1] - 1, all_ref.shape[2]
     box[...] = jnp.full(box.shape, -1.0, F32)
-    box[0 : length + 1, 0:tiles] = table_ref[...].astype(F32)
+    box[0 : length + 1, 0:tiles] = all_ref[me_ref[0]].astype(F32)
     rows = box[...]
     columns = rows.T
     earlier = iota((LANES, LANES), 1) < iota((LANES, LANES), 0)
@@ -294,7 +294,7 @@
             turned[part, number] = value.T
 
     across = [iota((8, LANES), 0).astype(F32) + 8.0 * xh for xh in range(2)]
-    unroll = 4
+    unroll = 8
 
     def composite(part, pixel_rows):
         def steps(n, carry):
@@ -450,7 +450,8 @@
 
 
 RUN = 5
-HALVES = (slice(0, 8), slice(8, 16))
+WIDE = 15
+HALVES = (slice(0, 16),)
 
 
 def target_kernel(target_ref, up_ref, down_ref, late_ref, out_ref, fields, tall):
@@ -475,8 +476,8 @@
                 for f in range(2):
                     tall[f, :, span(RUN * run + u + 1)] = down_columns(fields, u, f)
 
-        for first in range(0, spans, RUN):
-            count = RUN
+        for first in range(0, spans, WIDE):
+            count = WIDE
             for rows in HALVES:
                 for f, value in enumerate(across_rows(tall, rows, first, count)):
                     out_ref[f, c, rows, LANES * first : LANES * (first + count)] = value
@@ -554,8 +555,8 @@
                 for f in range(3):
                     tall[f, :, span(RUN * run + u + 1)] = down_columns(fields, u, f)
 
-        for first in range(0, spans, RUN):
-            count = RUN
+        for first in range(0, spans, WIDE):
+            count = WIDE
             lanes = slice(LANES * first, LANES * (first + count))
             for rows in HALVES:
                 mx, xx, xy = across_rows(tall, rows, first, count)
@@ -653,10 +654,10 @@
     route, code = call(
         functools.partial(route_kernel, cells, blocks, cap, rcap, per_row),
         (shape((8, LANES), jnp.int32), shape((devices, LANES), jnp.int32)),
-        [SMEM, VMEM, VMEM, pl.ANY],
+        [SMEM, VMEM, pl.ANY],
         [VMEM((LANES, LANES), F32), VMEM((devices, LANES), F32)],
         8, work,
-    )(me, own_table, table, target_head)
+    )(me, table, target_head)
     tile_rows = call(
         functools.partial(combine_kernel, tiles),
         shape((cells * 10 * rcap, LANES), F32),

time: 96 us -> 92.6 us (0.965)
  Pallas kernels: 40.5 us -> 35.3 us
  waiting for transfers between devices: 23.9 us -> 25.7 us
    pallas_call x1, Pallas kernels: 11.1 us -> 8.51 us  [local(): call(functools.partial(finish_kernel, groups, rcap, per_row), (planes, sh...]
    pallas_call x1, Pallas kernels: 3.85 us -> 2.06 us  [local(): call(target_kernel, shape((2, 3, 16, width), F32), [VMEM] * 3 + [pl.ANY],...]
    all_to_all x1, waiting for transfers between devices: 13.6 us -> 15.4 us  [local(): lax.all_to_all(tile_rows.reshape(cells, 10 * rcap, LANES), 'cell', split_...]
  transfers between devices with their start and end apart: 5 -> 5, of which waited for: 3 -> 3; matrix products, arithmetic and copies ran while one was open for 0% -> 0% of each run, Pallas kernels for 12% -> 10%
where the time goes in v4:
time: 92.6 us; the launch traced here: 92.1 us
  Pallas kernels  35.3 us (38%)
  starting transfers between devices  26.3 us (28%)
  waiting for transfers between devices  25.7 us (28%)
  local copies, waits for them, and re-layouts  3.3 us (4%)
    all_to_all x1, waiting for transfers between devices, local(): lax.all_to_all(tile_rows.reshape(cells, 10 * rcap, LANES), 'cell', split_...  15.4 us
    pallas_call x1, Pallas kernels, local(): call(functools.partial(render_kernel, cells, groups, cap, per_row, blocks...  13.8 us
    ppermute x1, waiting for transfers between devices, local(): target_up = lax.ppermute(target_tail, 'cell', down_pairs)  9.58 us
    pallas_call x1, Pallas kernels, local(): call(functools.partial(finish_kernel, groups, rcap, per_row), (planes, sh...  8.51 us
    all_to_all x1, starting transfers between devices, local(): lax.all_to_all(jnp.broadcast_to(own_table, (devices, length + 1, tiles)),...  7.3 us
    pallas_call x1, Pallas kernels, local(): call(prepare_kernel, shape((visible.shape[0], 9, rows, GBLK), F32), [SMEM...  6.37 us
    all_to_all x1, starting transfers between devices, local(): lax.all_to_all(made, ('cell', 'view'), split_axis=0, concat_axis=0, tiled...  5.84 us
    ppermute x1, starting transfers between devices, local(): target_down = lax.ppermute(target_head, 'cell', up_pairs)  5.76 us
  transfers between devices with their start and end apart: 5, of which 3 were waited for; matrix products, arithmetic and copies ran while one was open for 0% of the time, Pallas kernels for 10%

profile of v4, /device:TPU:0, one launch (start us, length us, event | category | flops | bytes accessed | tf_op | source)
XLA Modules:
  0.0 92.1 jit_solution(8533904034204838815)
XLA Ops:
  0.6 0.0 copy-start
  0.6 0.8 pad_add_fusion
  1.4 0.6 broadcast_in_dim.3
  2.0 7.3 %all-to-all-start = ((s32[32,3,120]{2,1,0:T(4,128)}), s32[32,3,120]{2,1,0:T(4,128)S(1)}, u32[]{:S(2)}, u32[]{:S(2)}) async-start(s32[32,3,120]{2,1,0:T(4,128)} %broadcast_in_dim.3), calls=%async_computation | async-start | bytes 131072 | tf_op jit(solution)/shard_map/all_to_all | solution.py:612
  9.4 0.1 stack.31.me_ref
  9.4 0.0 copy-start.1
  9.4 1.0 %copy-done.1 = s32[4,19200]{1,0:T(4,128)S(1)} copy-done((s32[4,19200]{1,0:T(4,128)S(1)}, s32[4,19200]{1,0:T(4,128)}, u32[]{:S(2)}) %copy-start.1) | copy-done | bytes 307224
  10.4 0.0 copy-start.2
  10.4 0.7 copy-done.2
  11.1 6.4 %shard_map.77.feats_ref = f32[4,9,160,128]{3,2,1,0:T(8,128)S(1)} custom-call(f32[4,15]{1,0:T(4,128)S(1)} %copy-done.2, f32[59,19200]{1,0:T(8,128)} %params_hbm.1, s32[4,19200]{1,0:T(4,128)S(1)} %copy-done.1), custom_call_target="tpu_custom_call" | custom-call | flops 192000000 | tf_op jit(solution)/shard_map/pallas_call | solution.py:617
  17.5 0.0 all-to-all-done.table_ref.all_ref
  17.5 0.0 copy-done
  17.5 13.8 %shard_map.78 = (f32[32,40,128]{2,1,0:T(8,128)}, f32[3,5,1920]{2,1,0:T(8,128)}, f32[3,5,1920]{2,1,0:T(8,128)}) custom-call(s32[5]{0:T(128)S(1)} %stack.31.me_ref, s32[32,3,120]{2,1,0:T(4,128)S(1)} %all-to-all-done.table_ref.all_ref, f32[4,9,160,128]{3,2,1,0:T(8,128)S(1)} %shard_map.77.feats_ref, f32[1,3,16,1920]{3,2,1,0:T(8,128)S(1)} %copy-done), custom_call_target="tpu_custom_call" | custom-call | flops 192000000 | tf_op jit(solution)/shard_map/pallas_call | solution.py:631
  31.3 5.8 %all-to-all-start.1 = ((f32[32,40,128]{2,1,0:T(8,128)}), f32[32,40,128]{2,1,0:T(8,128)S(1)}, u32[]{:S(2)}, u32[]{:S(2)}) async-start(f32[32,40,128]{2,1,0:T(8,128)} %get-tuple-element.10), calls=%async_computation.1 | async-start | bytes 1310720 | tf_op jit(solution)/shard_map/all_to_all | solution.py:652
  37.1 3.7 %collective-permute-start = (f32[3,5,1920]{2,1,0:T(8,128)}, f32[3,5,1920]{2,1,0:T(8,128)S(1)}, u32[]{:S(2)}, u32[]{:S(2)}) collective-permute-start(f32[3,5,1920]{2,1,0:T(8,128)} %get-tuple-element.11), channel_id=1, source_target_pairs={{0,2},{2,4},{4,6},{8,10},{10,12},{12,14},{14,16},{16,18},{18,20},{... | collective-permute-start | bytes 345608 | tf_op jit(solution)/shard_map/ppermute | solution.py:650
  40.8 5.8 %collective-permute-start.1 = (f32[3,5,1920]{2,1,0:T(8,128)}, f32[3,5,1920]{2,1,0:T(8,128)S(1)}, u32[]{:S(2)}, u32[]{:S(2)}) collective-permute-start(f32[3,5,1920]{2,1,0:T(8,128)} %get-tuple-element.7.late_ref), channel_id=1, source_target_pairs={{2,0},{4,2},{6,4},{10,8},{12,10},{14,12},{16,14},{18,16},{20,18},{... | collective-permute-start | bytes 345608 | tf_op jit(solution)/shard_map/ppermute | solution.py:651
  46.6 0.0 copy-start.3
  46.6 0.9 %copy-done.3 = f32[3,5,1920]{2,1,0:T(8,128)S(1)} copy-done((f32[3,5,1920]{2,1,0:T(8,128)S(1)}, f32[3,5,1920]{2,1,0:T(8,128)}, u32[]{:S(2)}) %copy-start.3) | copy-done | bytes 115224
  47.5 1.2 %shard_map.79 = (s32[8,128]{1,0:T(8,128)S(1)}, s32[32,128]{1,0:T(8,128)S(1)}) custom-call(s32[5]{0:T(128)S(1)} %stack.31.me_ref, s32[32,3,120]{2,1,0:T(4,128)S(1)} %all-to-all-done.table_ref.all_ref, f32[3,5,1920]{2,1,0:T(8,128)S(1)} %copy-done.3), custom_call_target="tpu_custom_call" | custom-call | flops 192000000 | tf_op jit(solution)/shard_map/pallas_call | solution.py:654
  48.7 9.6 %collective-permute-done.early_up.up_ref.target_up = f32[3,5,1920]{2,1,0:T(8,128)S(1)} collective-permute-done((f32[3,5,1920]{2,1,0:T(8,128)}, f32[3,5,1920]{2,1,0:T(8,128)S(1)}, u32[]{:S(2)}, u32[]{:S(2)}) %collective-permute-start) | collective-permute-done | bytes 115232 | tf_op jit(solution)/shard_map/ppermute | solution.py:650
  58.3 0.0 collective-permute-done.1.early_down.down_ref.target_down
  58.3 0.7 all-to-all-done.1
  59.0 3.4 %shard_map.80.late_ref = f32[1280,128]{1,0:T(8,128)} custom-call(s32[8,128]{1,0:T(8,128)S(1)} %get-tuple-element.9.route_ref, f32[1280,128]{1,0:T(8,128)S(1)} %bitcast.11, f32[3,5,1920]{2,1,0:T(8,128)S(1)} %collective-permute-done.early_up.up_ref.target_up, f32[3,5,1920]{2,1,0:T(8,128)S(1)} %collective-permute-done.1.early_down.down_ref.target_down), custom_call_target="tpu_custom_call" | custom-call | tf_op jit(solution)/shard_map/pallas_call | solution.py:661
  62.3 3.7 %all-to-all-start.2 = ((f32[16,80,128]{2,1,0:T(8,128)}), f32[16,80,128]{2,1,0:T(8,128)S(1)}, u32[]{:S(2)}, u32[]{:S(2)}) async-start(f32[16,80,128]{2,1,0:T(8,128)} %bitcast.9), calls=%async_computation.2 | async-start | bytes 1310720 | tf_op jit(solution)/shard_map/all_to_all | solution.py:666
  66.1 2.1 %shard_map.81.fixed_ref = f32[2,3,16,1920]{3,2,1,0:T(8,128)S(1)} custom-call(f32[1,3,16,1920]{3,2,1,0:T(8,128)S(1)} %copy-done, f32[3,5,1920]{2,1,0:T(8,128)S(1)} %collective-permute-done.early_up.up_ref.target_up, f32[3,5,1920]{2,1,0:T(8,128)S(1)} %collective-permute-done.1.early_down.down_ref.target_down, f32[1280,128]{1,0:T(8,128)} %shard_map.80.late_ref), custom_call_target="tpu_custom_call" | custom-call | flops 192000000 | tf_op jit(solution)/shard_map/pallas_call | solution.py:669
  68.1 15.4 %all-to-all-done.2.got_ref = f32[16,80,128]{2,1,0:T(8,128)S(1)} async-done(((f32[16,80,128]{2,1,0:T(8,128)}), f32[16,80,128]{2,1,0:T(8,128)S(1)}, u32[]{:S(2)}, u32[]{:S(2)}) %all-to-all-start.2) | async-done | bytes 655392 | tf_op jit(solution)/shard_map/all_to_all | solution.py:666
  83.6 8.5 %shard_map.82 = (f32[1,3,16,1920]{3,2,1,0:T(8,128)}, f32[1,16,1920]{2,1,0:T(8,128)}) custom-call(s32[32,128]{1,0:T(8,128)S(1)} %get-tuple-element.8.code_ref, s32[5]{0:T(128)S(1)} %stack.31.me_ref, f32[16,80,128]{2,1,0:T(8,128)S(1)} %all-to-all-done.2.got_ref, f32[1,3,16,1920]{3,2,1,0:T(8,128)S(1)} %copy-done, f32[2,3,16,1920]{3,2,1,0:T(8,128)S(1)} %shard_map.81.fixed_ref, ...), custom_call_target="tpu_custom_call" | custom-call | tf_op jit(solution)/shard_map/pallas_call | solution.py:676
Async XLA Ops:
  0.6 16.8 %copy-start = (f32[1,3,16,1920]{3,2,1,0:T(8,128)S(1)}, f32[1,3,16,1920]{3,2,1,0:T(8,128)}, u32[]{:S(2)}) copy-start(f32[1,3,16,1920]{3,2,1,0:T(8,128)} %target_ref.5) | copy-start | bytes 1105924
  2.0 15.4 %all-to-all-start = ((s32[32,3,120]{2,1,0:T(4,128)}), s32[32,3,120]{2,1,0:T(4,128)S(1)}, u32[]{:S(2)}, u32[]{:S(2)}) async-start(s32[32,3,120]{2,1,0:T(4,128)} %broadcast_in_dim.3), calls=%async_computation | async-start | bytes 131072 | tf_op jit(solution)/shard_map/all_to_all | solution.py:612
  9.4 1.0 %copy-start.1 = (s32[4,19200]{1,0:T(4,128)S(1)}, s32[4,19200]{1,0:T(4,128)}, u32[]{:S(2)}) copy-start(s32[4,19200]{1,0:T(4,128)} %seen_hbm.1) | copy-start | bytes 921604
  10.4 0.7 copy-start.2
  31.3 27.7 %all-to-all-start.1 = ((f32[32,40,128]{2,1,0:T(8,128)}), f32[32,40,128]{2,1,0:T(8,128)S(1)}, u32[]{:S(2)}, u32[]{:S(2)}) async-start(f32[32,40,128]{2,1,0:T(8,128)} %get-tuple-element.10), calls=%async_computation.1 | async-start | bytes 1310720 | tf_op jit(solution)/shard_map/all_to_all | solution.py:652
  37.1 21.2 %collective-permute-start = (f32[3,5,1920]{2,1,0:T(8,128)}, f32[3,5,1920]{2,1,0:T(8,128)S(1)}, u32[]{:S(2)}, u32[]{:S(2)}) collective-permute-start(f32[3,5,1920]{2,1,0:T(8,128)} %get-tuple-element.11), channel_id=1, source_target_pairs={{0,2},{2,4},{4,6},{8,10},{10,12},{12,14},{14,16},{16,18},{18,20},{... | collective-permute-start | bytes 345608 | tf_op jit(solution)/shard_map/ppermute | solution.py:650
  40.8 17.5 %collective-permute-start.1 = (f32[3,5,1920]{2,1,0:T(8,128)}, f32[3,5,1920]{2,1,0:T(8,128)S(1)}, u32[]{:S(2)}, u32[]{:S(2)}) collective-permute-start(f32[3,5,1920]{2,1,0:T(8,128)} %get-tuple-element.7.late_ref), channel_id=1, source_target_pairs={{2,0},{4,2},{6,4},{10,8},{12,10},{14,12},{16,14},{18,16},{20,18},{... | collective-permute-start | bytes 345608 | tf_op jit(solution)/shard_map/ppermute | solution.py:651
  46.6 0.9 %copy-start.3 = (f32[3,5,1920]{2,1,0:T(8,128)S(1)}, f32[3,5,1920]{2,1,0:T(8,128)}, u32[]{:S(2)}) copy-start(f32[3,5,1920]{2,1,0:T(8,128)} %get-tuple-element.7.late_ref) | copy-start | bytes 345604
  62.3 21.2 %all-to-all-start.2 = ((f32[16,80,128]{2,1,0:T(8,128)}), f32[16,80,128]{2,1,0:T(8,128)S(1)}, u32[]{:S(2)}, u32[]{:S(2)}) async-start(f32[16,80,128]{2,1,0:T(8,128)} %bitcast.9), calls=%async_computation.2 | async-start | bytes 1310720 | tf_op jit(solution)/shard_map/all_to_all | solution.py:666
